TPU v7x, 128 devices: a whole 4x4x4 slice. The times are simulated.
128 devices in a mesh: dp: 16 (over z_hi, x, core), feat: 8 (over z_lo, y).
Axes of the slice: x: 4, y: 4, z: 4 (z_hi: 2, z_lo: 2; z = z_hi * 2 + z_lo), core: 2. Of those that a mesh axis runs over, the one named last changes fastest.
Arguments:
- view_features: bfloat16 [2, 2048, 8192], P(None, 'dp', 'feat'), may hold values from 0 to 55, as said below
- weight: float32 [8192, 8192], P('dp', 'feat'), may hold values from -64 to 64
- velocity: float32 [8192, 8192], P('dp', 'feat'), may hold values from -6 to 6
Outputs:
- new_weight: float32 [8192, 8192], P('dp', 'feat')
- new_velocity: float32 [8192, 8192], P('dp', 'feat')
Inputs may be any that keep to these rules, and one draw needn't show every extreme that they name: `view_features`: nonnegative features.
All inputs are finite; a program needn't handle non-finite values.
Results may differ from a plain program's by a relative error of at most 0.039.
Values may be sent and summed in bfloat16 or wider, within the bound.
A program may use at most 128 MiB of HBM per device.

v0:
```python
import jax
import jax.numpy as jnp
from jax import lax
from jax.sharding import PartitionSpec as P

EPSILON = 1e-05
NORM_EPSILON = 1e-06
REDUNDANCY = 0.0051
MOMENTUM = 0.9
LEARN_RATE = 0.2


def per_device(view_features, weight, velocity):
    images_dev = view_features.shape[1]
    feat_width = view_features.shape[2]
    dp_width = weight.shape[0]
    batch_total = images_dev * lax.axis_size("dp")
    dp_index = lax.axis_index("dp")
    feat_index = lax.axis_index("feat")
    view_rows = lax.all_gather(view_features, "feat", axis=2, tiled=True)
    columns = lax.all_to_all(view_rows, "dp", split_axis=2, concat_axis=1, tiled=True)
    weight_half = weight.astype(jnp.bfloat16)
    block_rows = columns
    outputs = lax.psum_scatter(
        jnp.einsum(
            "vnk,kf->nvf", block_rows, weight_half, preferred_element_type=jnp.float32
        ).astype(jnp.bfloat16),
        "dp",
        scatter_dimension=0,
        tiled=True,
    ).astype(jnp.float32)
    average = lax.psum(jnp.sum(outputs, 0), "dp") / batch_total
    centered = outputs - average
    variance = lax.psum(jnp.sum(centered * centered, 0), "dp") / batch_total
    inverse = lax.rsqrt(variance + EPSILON)
    normed = centered * inverse
    normed_half = normed.astype(jnp.bfloat16)
    first_rows = normed_half[:, 0]
    second_all = lax.all_gather(normed_half[:, 1], "dp", axis=0, tiled=True)
    first_wide = lax.all_gather(first_rows, "feat", axis=1, tiled=True)
    first_cols = lax.all_to_all(first_wide, "dp", split_axis=1, concat_axis=0, tiled=True)
    correlation = (
        jnp.einsum("nk,nf->kf", first_cols, second_all, preferred_element_type=jnp.float32)
        / batch_total
    )
    row_ids = dp_index * dp_width + lax.broadcasted_iota(jnp.int32, (dp_width, feat_width), 0)
    col_ids = feat_index * feat_width + lax.broadcasted_iota(jnp.int32, (dp_width, feat_width), 1)
    diagonal = row_ids == col_ids
    scaled = (
        jnp.where(diagonal, -2.0 * (1.0 - correlation), 2.0 * REDUNDANCY * correlation)
        / batch_total
    ).astype(jnp.bfloat16)
    first_part = jnp.einsum(
        "nf,kf->nk", second_all, scaled, preferred_element_type=jnp.float32
    ).astype(jnp.bfloat16)
    exchanged = lax.all_to_all(first_part, "dp", split_axis=0, concat_axis=1, tiled=True)
    first_grad = lax.psum_scatter(exchanged, "feat", scatter_dimension=1, tiled=True).astype(
        jnp.float32
    )
    block_rows = first_cols
    second_grad = lax.psum_scatter(
        jnp.dot(block_rows, scaled, preferred_element_type=jnp.float32).astype(jnp.bfloat16),
        "dp",
        scatter_dimension=0,
        tiled=True,
    ).astype(jnp.float32)
    feature_grads = jnp.stack([first_grad, second_grad], 1)
    grad_sum, grad_cross = lax.psum(
        (jnp.sum(feature_grads, 0), jnp.sum(feature_grads * normed, 0)), "dp"
    )
    out_grad = (
        inverse * (feature_grads - grad_sum / batch_total - normed * (grad_cross / batch_total))
    ).astype(jnp.bfloat16)
    weight_grad = jnp.einsum(
        "vnk,nvf->kf",
        columns,
        lax.all_gather(out_grad, "dp", axis=0, tiled=True),
        preferred_element_type=jnp.float32,
    )
    weight_local = jnp.sum(weight * weight)
    grad_local = jnp.sum(weight_grad * weight_grad)
    weight_sq, grad_sq = lax.psum((weight_local, grad_local), ("dp", "feat"))
    trust = jnp.sqrt(weight_sq) / (jnp.sqrt(grad_sq) + NORM_EPSILON)
    new_velocity = MOMENTUM * velocity + trust * weight_grad
    new_weight = weight - LEARN_RATE * new_velocity
    return (new_weight, new_velocity)


def solution(mesh):
    in_specs = (P(None, "dp", "feat"), P("dp", "feat"), P("dp", "feat"))
    out_specs = (P("dp", "feat"), P("dp", "feat"))
    return jax.shard_map(
        per_device, mesh=mesh, in_specs=in_specs, out_specs=out_specs, check_vma=False
    )
```

profile of v0, /device:TPU:1, one launch (start us, length us, event | category | flops | bytes accessed | tf_op | source)
XLA Modules:
  0.0 817.5 jit_solution(9866836204159298861)
XLA Ops:
  9.3 56.8 %all-gather.7.cloned.1.call-done = bf16[2,128,8192]{1,0,2:T(2,128)(2,1)} async-done(((bf16[2,128,1024]{1,0,2:T(2,128)(2,1)}), bf16[2,128,8192]{1,0,2:T(2,128)(2,1)}) %all-gather.7.cloned.1.call-update) | async-done | bytes 4194320 | tf_op jit(solution)/shard_map/all_gather | solution.py:20
  66.1 58.0 %all_to_all.56 = bf16[2,128,8192]{1,0,2:T(2,128)(2,1)} all-to-all(bf16[2,128,8192]{1,0,2:T(2,128)(2,1)} %all-gather.7.cloned.1.call-done), channel_id=1, replica_groups=mesh['dp'=16,'feat'=8] {'dp'}, dimensions={2} | all-to-all | bytes 8388608 | tf_op jit(solution)/shard_map/all_to_all | solution.py:21
  124.2 11.3 %copy.34 = bf16[2,128,16,512]{3,1,2,0:T(8,128)(2,1)} copy(bf16[2,128,16,512]{1,0,3,2:T(2,128)(2,1)} %bitcast.50) | data formatting | bytes 8388608 | tf_op jit(solution)/shard_map/all_to_all | solution.py:21
  135.5 9.0 %convolution_convert_fusion = bf16[1024,2,2048]{2,0,1:T(8,128)(2,1)} fusion(bf16[2,2048,512]{2,1,0:T(8,128)(2,1)} %bitcast.54, f32[512,1024]{1,0:T(8,128)S(1)} %copy-done), kind=kOutput, calls=%fused_computation | convolution fusion | flops 4299685888 | bytes 14680064 | tf_op jit(solution)/shard_map/vnk,kf->nvf/dot_general | solution.py:25
  144.4 12.3 %copy.48 = bf16[2048,2048]{1,0:T(8,128)(2,1)} copy(bf16[2048,2048]{0,1:T(8,128)(2,1)} %bitcast.51) | data formatting | bytes 16777216
  156.8 96.2 %reduce-scatter.10.cloned.1.call-done = bf16[128,2048]{1,0:T(8,128)(2,1)} async-done(((bf16[2048,2048]{1,0:T(8,128)(2,1)}), bf16[128,2048]{1,0:T(8,128)(2,1)}) %reduce-scatter.10.cloned.1.call-update) | async-done | bytes 524304
  254.6 35.0 %psum.43 = f32[2,1024]{1,0:T(2,128)S(1)} all-reduce(f32[2,1024]{1,0:T(2,128)S(1)} %convert_reduce_fusion.1), channel_id=1, replica_groups=mesh['dp'=16,'feat'=8] {'dp'}, use_global_device_ids=true, to_apply=%region_4.0 | all-reduce | flops 2048 | bytes 16384 | tf_op jit(solution)/shard_map/psum | solution.py:32
  290.2 33.7 %psum.44 = f32[2,1024]{1,0:T(2,128)S(1)} all-reduce(f32[2,1024]{1,0:T(2,128)S(1)} %fusion.17), channel_id=1, replica_groups=mesh['dp'=16,'feat'=8] {'dp'}, use_global_device_ids=true, to_apply=%region_6.7 | all-reduce | flops 2048 | bytes 16384 | tf_op jit(solution)/shard_map/psum | solution.py:34
  325.9 34.9 %all-gather.13.cloned.1.call-done = bf16[128,1,8192]{0,2,1:T(8,128)(2,1)} async-done(((bf16[128,1,1024]{0,2,1:T(8,128)(2,1)}), bf16[128,1,8192]{0,2,1:T(8,128)(2,1)}) %all-gather.13.cloned.1.call-update) | async-done | bytes 2097168 | tf_op jit(solution)/shard_map/all_gather | solution.py:40
  360.8 3.9 copy.36
  364.7 11.9 %all-to-all-start.1 = ((bf16[128,16,512]{2,0,1:T(8,128)(2,1)}), bf16[128,16,512]{2,0,1:T(8,128)(2,1)}, u32[]{:S(2)}, u32[]{:S(2)}) async-start(bf16[128,16,512]{2,0,1:T(8,128)(2,1)} %copy.36), calls=%async_computation.1 | async-start | bytes 4194304 | tf_op jit(solution)/shard_map/all_to_all | solution.py:41
  376.7 32.8 %all-to-all-done.1 = bf16[128,16,512]{2,0,1:T(8,128)(2,1)} async-done(((bf16[128,16,512]{2,0,1:T(8,128)(2,1)}), bf16[128,16,512]{2,0,1:T(8,128)(2,1)}, u32[]{:S(2)}, u32[]{:S(2)}) %all-to-all-start.1) | async-done | bytes 2097184 | tf_op jit(solution)/shard_map/all_to_all | solution.py:41
  409.6 31.4 %all-gather.11.cloned.1.call-done = bf16[2048,1,1024]{0,2,1:T(8,128)(2,1)} async-done(((bf16[128,1,1024]{0,2,1:T(8,128)(2,1)}), bf16[2048,1,1024]{0,2,1:T(8,128)(2,1)}) %all-gather.11.cloned.1.call-update) | async-done | bytes 4194320 | tf_op jit(solution)/shard_map/all_gather | solution.py:39
  441.0 5.2 fusion.2
  447.5 6.0 convolution_convert_fusion.1
  453.8 5.6 fusion.4
  459.4 32.0 %all_to_all.57 = bf16[16,128,512]{2,1,0:T(8,128)(2,1)} all-to-all(bf16[16,128,512]{2,1,0:T(8,128)(2,1)S(1)} %bitcast.59), channel_id=1, replica_groups=mesh['dp'=16,'feat'=8] {'dp'}, dimensions={0} | all-to-all | bytes 4194304 | tf_op jit(solution)/shard_map/all_to_all | solution.py:56
  495.4 35.6 %reduce-scatter.12.cloned.1.call-done = bf16[128,1024]{1,0:T(8,128)(2,1)} async-done(((bf16[2048,1024]{1,0:T(8,128)(2,1)}), bf16[128,1024]{1,0:T(8,128)(2,1)}) %reduce-scatter.12.cloned.1.call-update) | async-done | bytes 262160
  532.0 39.2 %reduce-scatter.8.cloned.1.call-done = bf16[128,1024]{0,1:T(8,128)(2,1)} async-done(((bf16[128,8192]{0,1:T(8,128)(2,1)}), bf16[128,1024]{0,1:T(8,128)(2,1)}) %reduce-scatter.8.cloned.1.call-update) | async-done | bytes 262160 | tf_op jit(solution)/shard_map/reduce_scatter | solution.py:57
  573.3 64.8 %all-reduce.1 = (f32[2,1024]{1,0:T(2,128)S(1)}, f32[2,1024]{1,0:T(2,128)S(1)}) all-reduce(f32[2,1024]{1,0:T(2,128)S(1)} %get-tuple-element.11, f32[2,1024]{1,0:T(2,128)S(1)} %get-tuple-element.10), channel_id=1, replica_groups=mesh['dp'=16,'feat'=8] {'dp'}, use_global_device_ids=true, to_apply=%region_12.13 | all-reduce | flops 4096 | bytes 32768 | tf_op jit(solution)/shard_map/psum | solution.py:68
  647.5 76.8 %all-gather.9.cloned.1.call-done = bf16[2048,2,1024]{0,2,1:T(8,128)(2,1)} async-done(((bf16[128,2,1024]{0,2,1:T(8,128)(2,1)}), bf16[2048,2,1024]{0,2,1:T(8,128)(2,1)}) %all-gather.9.cloned.1.call-update) | async-done | bytes 8388624 | tf_op jit(solution)/shard_map/all_gather | solution.py:77
  724.2 11.0 %fusion.7 = (f32[]{:T(128)}, f32[1024,512,1]{1,0,2:T(8,128)}) fusion(bf16[2048,2,1024]{0,2,1:T(8,128)(2,1)} %all-gather.9.cloned.1.call-done, bf16[2,2048,512]{2,1,0:T(8,128)(2,1)} %bitcast.55), kind=kOutput, calls=%fused_computation.10 | convolution fusion | flops 4296015872 | bytes 14680068 | tf_op jit(solution)/shard_map/vnk,nvf->kf/dot_general | solution.py:74
  735.3 64.2 %all-reduce = (f32[]{:T(128)}, f32[]{:T(128)}) all-reduce(f32[]{:T(128)} %multiply_reduce_fusion, f32[]{:T(128)} %get-tuple-element.20), channel_id=1, replica_groups=mesh['dp'=16,'feat'=8] {'dp','feat'}, use_global_device_ids=true, to_apply=%region_1.0 | all-reduce | flops 2 | bytes 16 | tf_op jit(solution)/shard_map/psum | solution.py:82
  800.8 5.0 multiply_subtract_fusion
  (42 shorter events, 29.3 us)
Async XLA Ops:
  7.2 59.0 %all-gather.7.cloned.1.call-start = ((), (), s32[]{:S(2)}) async-start(), calls=%async_computation.6 | async-start | bytes 4718592 | tf_op jit(solution)/shard_map/all_gather | solution.py:20
  9.2 243.8 %reduce-scatter.10.cloned.1.call-start = ((), (), s32[]{:S(2)}) async-start(), calls=%async_computation.11 | async-start | bytes 8912896
  124.2 11.3 %copy-start = (f32[512,1024]{1,0:T(8,128)S(1)}, f32[512,1024]{1,0:T(8,128)}, u32[]{:S(2)}) copy-start(f32[512,1024]{1,0:T(8,128)} %param.4) | copy-start | bytes 6291460
  156.8 204.0 %all-gather.13.cloned.1.call-start = ((), (), s32[]{:S(2)}) async-start(), calls=%async_computation.10 | async-start | bytes 2359296 | tf_op jit(solution)/shard_map/all_gather | solution.py:40
  325.4 115.7 %all-gather.11.cloned.1.call-start = ((), (), s32[]{:S(2)}) async-start(), calls=%async_computation.9 | async-start | bytes 4456448 | tf_op jit(solution)/shard_map/all_gather | solution.py:39
  364.7 44.8 %all-to-all-start.1 = ((bf16[128,16,512]{2,0,1:T(8,128)(2,1)}), bf16[128,16,512]{2,0,1:T(8,128)(2,1)}, u32[]{:S(2)}, u32[]{:S(2)}) async-start(bf16[128,16,512]{2,0,1:T(8,128)(2,1)} %copy.36), calls=%async_computation.1 | async-start | bytes 4194304 | tf_op jit(solution)/shard_map/all_to_all | solution.py:41
  376.7 154.2 %reduce-scatter.12.cloned.1.call-start = ((), (), s32[]{:S(2)}) async-start(), calls=%async_computation.12 | async-start | bytes 4456448
  446.2 1.3 copy-start.3
  453.6 117.6 %reduce-scatter.8.cloned.1.call-start = ((), (), s32[]{:S(2)}) async-start(), calls=%async_computation.7 | async-start | bytes 2359296 | tf_op jit(solution)/shard_map/reduce_scatter | solution.py:57
  495.3 228.9 %all-gather.9.cloned.1.call-start = ((), (), s32[]{:S(2)}) async-start(), calls=%async_computation.8 | async-start | bytes 8912896 | tf_op jit(solution)/shard_map/all_gather | solution.py:77
  647.4 153.4 %copy-start.1 = (f32[512,1024]{0,1:T(8,128)S(1)}, f32[512,1024]{0,1:T(8,128)}, u32[]{:S(2)}) copy-start(f32[512,1024]{0,1:T(8,128)} %copy.39) | copy-start | bytes 6291460
  805.8 3.0 copy-start.2
Sparse Core Ops, SparseCore 0:
  10.2 55.8 all-gather.6
  156.9 96.0 reduce-scatter.9
  325.5 35.3 all-gather.12
  363.5 77.4 all-gather.10
  453.7 77.1 reduce-scatter.11
  533.9 37.3 reduce-scatter.7
  641.7 82.4 all-gather.8
where the time goes:
time: 819 us; the launch traced here: 818 us
  waiting for transfers between devices  404 us (49%)
  blocking collectives  288 us (35%)
  local copies, waits for them, and re-layouts  47.6 us (6%)
  matrix products  36.8 us (4%)
  between operations  15.6 us (2%)
  other arithmetic  13.1 us (2%)
  starting transfers between devices  12.4 us (2%)
    unnamed x9, waiting for transfers between devices  132 us
    all_gather x1, waiting for transfers between devices, per_device(): lax.all_gather(out_grad, 'dp', axis=0, tiled=True)  76.8 us
    psum x1, blocking collectives, per_device(): lax.psum((jnp.sum(feature_grads, 0), jnp.sum(feature_grads * normed, 0)),...  64.8 us
    psum x1, blocking collectives, per_device(): weight_sq, grad_sq = lax.psum((weight_local, grad_local), ('dp', 'feat'))  64.2 us
    all_to_all x1, blocking collectives, per_device(): lax.all_to_all(view_rows, 'dp', split_axis=2, concat_axis=1, tiled=True)  58 us
    all_gather x1, waiting for transfers between devices, per_device(): view_rows = lax.all_gather(view_features, 'feat', axis=2, tiled=True)  56.8 us
    reduce_scatter x1, waiting for transfers between devices, per_device(): lax.psum_scatter(exchanged, 'feat', scatter_dimension=1, tiled=True)  39.2 us
    psum x1, blocking collectives, per_device(): average = lax.psum(jnp.sum(outputs, 0), 'dp') / batch_total  35 us
  transfers between devices with their start and end apart: 8, of which 8 were waited for; matrix products, arithmetic and copies ran while one was open for 2% of the time, Pallas kernels for 0%

commit v1 on v0

v1 whole, which is shorter than its diff:
```python
import functools

import jax
import jax.numpy as jnp
from jax import lax
from jax.experimental import pallas as pl
from jax.experimental.pallas import tpu as pltpu
from jax.sharding import PartitionSpec as P

EPSILON = 1e-05
NORM_EPSILON = 1e-06
REDUNDANCY = 0.0051
MOMENTUM = 0.9
LEARN_RATE = 0.2
MESH = pl.DeviceIdType.MESH
BF = jnp.bfloat16
F32 = jnp.float32
NCH = 4


class Place:
    def __init__(self):
        d, f = lax.axis_index("dp"), lax.axis_index("feat")
        self.d, self.f, self.p = d, f, d // 2
        self.zh, self.x, self.c = d // 8, (d // 2) % 4, d % 2
        self.zl, self.y = f // 4, f % 4

    def at(self, zh=None, x=None, c=None, zl=None, y=None):
        zh = self.zh if zh is None else zh
        x = self.x if x is None else x
        c = self.c if c is None else c
        zl = self.zl if zl is None else zl
        y = self.y if y is None else y
        return ((zh * 4 + x) * 2 + c, zl * 4 + y)


def signal(target):
    pl.semaphore_signal(
        pltpu.get_barrier_semaphore(), inc=1, device_id=target, device_id_type=MESH
    )


def remote(src, dst, send, recv, target):
    return pltpu.make_async_remote_copy(
        src_ref=src, dst_ref=dst, send_sem=send, recv_sem=recv, device_id=target, device_id_type=MESH
    )


class Gather:
    def __init__(self, q, r, device, piece, send, recv):
        up, down, far, other = (r + 1) % 4, (r + 3) % 4, (r + 2) % 4, 1 - q
        self.blocks = [
            other * 4 + r, q * 4 + down, q * 4 + up, q * 4 + far,
            other * 4 + down, other * 4 + up, other * 4 + far,
        ]
        mine = q * 4 + r

        def make(block, k, slot, target):
            ref = piece(block, k)
            return remote(ref, ref, send.at[slot, k], recv.at[slot, k], target)

        to_up, to_down, to_pair = device(q, up), device(q, down), device(other, r)
        self.copies = []
        for k in range(NCH):
            self.copies.append([
                make(mine, k, 0, to_pair),
                make(mine, k, 1, to_up),
                make(mine, k, 2, to_down),
                make(self.blocks[1], k, 3, to_up) if k % 2 == 0 else make(self.blocks[2], k, 3, to_down),
                make(self.blocks[0], k, 4, to_up),
                make(self.blocks[0], k, 5, to_down),
                make(self.blocks[3], k, 6, to_pair),
            ])

    def own(self, k):
        for slot in (0, 1, 2):
            self.copies[k][slot].start()

    def near(self, k):
        c = self.copies[k]
        c[0].wait_recv()
        c[4].start()
        c[5].start()
        c[1].wait_recv()
        c[2].wait_recv()
        c[3].start()

    def far(self, k):
        c = self.copies[k]
        c[3].wait_recv()
        c[6].start()

    def rest(self, k, slot):
        self.copies[k][slot].wait_recv()

    def close(self):
        for c in self.copies:
            for copy in c:
                copy.wait_send()


def forward_kernel(
    x_ref, w_ref, xg, normed_ref, half_ref, inv_ref,
    wf, ys, yr, zs, zr, yacc,
    perm_s, perm_r, w_s, w_r, ag_s, ag_r, rs_s, rs_r, z_s, z_r,
):
    me = Place()
    p, f, c, x, y, zh, zl = me.p, me.f, me.c, me.x, me.y, me.zh, me.zl
    same = f == p
    piece = 256 // NCH
    half = NCH // 2
    for v in range(2):
        @pl.when(jnp.logical_not(same & (c == v)))
        def _():
            signal((f * 2 + v, p))
    partners = [
        me.at(c=1 - c), me.at(y=(y + 1) % 4), me.at(y=(y + 3) % 4), me.at(zl=1 - zl),
        me.at(x=(x + 1) % 4), me.at(x=(x + 2) % 4), me.at(x=(x + 3) % 4), me.at(zh=1 - zh),
    ]
    for t in partners:
        signal(t)
    own_rows = pl.ds(pl.multiple_of(c * 512, 512), 512)
    wf[own_rows, :] = w_ref[...].astype(BF)
    pl.semaphore_wait(pltpu.get_barrier_semaphore(), len(partners) + jnp.where(same, 1, 2))

    def perm(v, h):
        src = x_ref.at[v, pl.ds(h * piece, piece)]
        dst = xg.at[p, pl.ds(pl.multiple_of((c * half + h) * piece, piece), piece)]
        return remote(src, dst, perm_s.at[v, h], perm_r.at[c * half + h], (f * 2 + v, p))

    for h in range(half):
        for v in range(2):
            here = same & (c == v)

            @pl.when(here)
            def _():
                pltpu.make_async_copy(
                    x_ref.at[v, pl.ds(h * piece, piece)],
                    xg.at[p, pl.ds(pl.multiple_of((c * half + h) * piece, piece), piece)],
                    perm_r.at[c * half + h],
                ).start()

            @pl.when(jnp.logical_not(here))
            def _():
                perm(v, h).start()

    wcopy = remote(wf.at[own_rows], wf.at[own_rows], w_s, w_r, me.at(c=1 - c))
    wcopy.start()

    ag = Gather(
        zl, y, lambda q, r: me.at(zl=q, y=r),
        lambda b, k: xg.at[b, pl.ds(k * piece, piece)], ag_s, ag_r,
    )
    for k in (0, 2, 1, 3):
        ref = xg.at[f, pl.ds(k * piece, piece)]
        pltpu.make_async_copy(ref, ref, perm_r.at[k]).wait()
        ag.own(k)
    wcopy.wait_recv()

    order = [f] + ag.blocks
    sends = []

    def product(o):
        b = order[o]

        @pl.loop(0, 4)
        def _(j):
            cols = pl.ds(pl.multiple_of(j * 256, 256), 256)
            part = jnp.dot(xg[b], wf[:, cols], preferred_element_type=F32).astype(BF)
            rows = pl.ds(pl.multiple_of(b * 256, 256), 256)
            ys[2 * (j % 2), j // 2, rows, :] = part[:, :128]
            ys[2 * (j % 2) + 1, j // 2, rows, :] = part[:, 128:]

        rows = pl.ds(pl.multiple_of(b * 256, 256), 256)
        for dx in (2, 1, 3):
            xt = (x + dx) % 4
            copy = remote(
                ys.at[xt, :, rows], yr.at[dx - 1, :, rows], rs_s.at[dx - 1, o], rs_r.at[dx - 1, o], me.at(x=xt)
            )
            copy.start()
            sends.append(copy)

    product(0)
    for k in (0, 2, 1, 3):
        ag.near(k)
    product(1)
    product(2)
    product(3)
    for k in range(NCH):
        ag.far(k)
    product(4)
    for k in range(NCH):
        ag.rest(k, 4)
    product(5)
    for k in range(NCH):
        ag.rest(k, 5)
    product(6)
    for k in range(NCH):
        ag.rest(k, 6)
    product(7)
    zcopies = []
    for o in range(8):
        rows = pl.ds(pl.multiple_of(order[o] * 256, 256), 256)
        for copy in sends[3 * o:3 * o + 3]:
            copy.wait_recv()

        def total(side):
            s = ys[x, side, rows, :].astype(F32)
            for i in range(3):
                s = s + yr[i, side, rows, :].astype(F32)
            return s

        zs[rows, :] = total(1 - zh).astype(BF)
        copy = remote(zs.at[rows], zr.at[rows], z_s.at[o], z_r.at[o], me.at(zh=1 - zh))
        copy.start()
        zcopies.append(copy)
        yacc[rows, :] = total(zh)
    for copy in zcopies:
        copy.wait_recv()
    outputs = yacc[...] + zr[...].astype(F32)
    average = jnp.sum(outputs, 0, keepdims=True) / 2048
    centered = outputs - average
    variance = jnp.sum(centered * centered, 0, keepdims=True) / 2048
    inverse = lax.rsqrt(variance + EPSILON)
    normed = centered * inverse
    normed_ref[...] = normed
    half_ref[...] = normed.astype(BF)
    inv_ref[...] = jnp.broadcast_to(inverse, (8, 128))
    for h in range(half):
        for v in range(2):
            @pl.when(jnp.logical_not(same & (c == v)))
            def _():
                perm(v, h).wait_send()
    wcopy.wait_send()
    ag.close()
    for copy in sends + zcopies:
        copy.wait_send()


def vmem(n):
    return [pl.BlockSpec(memory_space=pltpu.VMEM)] * n


def forward(view_features, weight):
    dma = pltpu.SemaphoreType.DMA
    return pl.pallas_call(
        forward_kernel,
        out_shape=(
            jax.ShapeDtypeStruct((8, 256, 1024), BF),
            jax.ShapeDtypeStruct((2048, 128), F32),
            jax.ShapeDtypeStruct((2048, 128), BF),
            jax.ShapeDtypeStruct((8, 128), F32),
        ),
        in_specs=vmem(2),
        out_specs=tuple(vmem(4)),
        scratch_shapes=[
            pltpu.VMEM((1024, 1024), BF),
            pltpu.VMEM((4, 2, 2048, 128), BF),
            pltpu.VMEM((3, 2, 2048, 128), BF),
            pltpu.VMEM((2048, 128), BF),
            pltpu.VMEM((2048, 128), BF),
            pltpu.VMEM((2048, 128), F32),
            dma((2, NCH // 2)), dma((NCH,)), dma, dma, dma((7, NCH)), dma((7, NCH)),
            dma((3, 8)), dma((3, 8)), dma((8,)), dma((8,)),
        ],
        compiler_params=pltpu.CompilerParams(
            collective_id=0, has_side_effects=True, vmem_limit_bytes=60 * 2**20
        ),
    )(view_features, weight)


def per_device(view_features, weight, velocity):
    d, f = lax.axis_index("dp"), lax.axis_index("feat")
    p, c = d // 2, d % 2
    xg, normed, half, inverse = forward(view_features, weight)
    swap = [(i, i ^ 1) for i in range(16)]
    group = [[q * 2 + k for q in range(8)] for k in range(2)]
    other = lax.ppermute(half, "dp", swap)
    n = 2048
    wide = lax.all_gather(half, "dp", axis=1, tiled=True, axis_index_groups=group)
    mine = lax.dynamic_slice_in_dim(wide, p * 256, 256, 0)
    part = lax.dot_general(mine, wide, (((1,), (1,)), ((), ())), preferred_element_type=F32).astype(BF)
    gram = lax.psum(part.astype(F32), "feat").astype(BF)
    gram = lax.ppermute(gram, "dp", swap)
    kappa = 2.0 * REDUNDANCY / (n * n)
    grads = (kappa * jnp.dot(gram, wide, preferred_element_type=F32)).astype(BF)
    grads = lax.all_to_all(grads, "dp", 1, 0, tiled=True, axis_index_groups=group).astype(F32)
    corr = jnp.sum(half.astype(F32) * other.astype(F32), 0) / n
    extra = (-2.0 * (1.0 - corr) - 2.0 * REDUNDANCY * corr) / n
    grads = grads + extra * other.astype(F32)
    mean = jnp.mean(grads, 0)
    cross = jnp.mean(grads * normed, 0)
    og = (inverse[0] * (grads - mean - normed * cross)).astype(BF)
    og = lax.all_gather(og, "dp", axis=1, tiled=True, axis_index_groups=group)
    wg = lax.dot_general(xg.reshape(2048, 1024), og, (((0,), (0,)), ((), ())), preferred_element_type=F32)
    keep = lax.dynamic_slice_in_dim(wg, c * 512, 512, 0)
    give = lax.dynamic_slice_in_dim(wg, (1 - c) * 512, 512, 0)
    wg = keep + lax.ppermute(give, "dp", swap)
    wsq, gsq = lax.psum((jnp.sum(weight * weight), jnp.sum(wg * wg)), ("dp", "feat"))
    trust = jnp.sqrt(wsq) / (jnp.sqrt(gsq) + NORM_EPSILON)
    new_velocity = MOMENTUM * velocity + trust * wg
    return weight - LEARN_RATE * new_velocity, new_velocity


def solution(mesh):
    in_specs = (P(None, "dp", "feat"), P("dp", "feat"), P("dp", "feat"))
    out_specs = (P("dp", "feat"), P("dp", "feat"))
    return jax.shard_map(
        per_device, mesh=mesh, in_specs=in_specs, out_specs=out_specs, check_vma=False
    )
```

time: 819 us -> 454 us (0.55)
  waiting for transfers between devices: 404 us -> 167 us
  blocking collectives: 288 us -> 127 us
  Pallas kernels: 0 us -> 94.5 us
  local copies, waits for them, and re-layouts: 47.6 us -> 4.36 us
  matrix products: 36.8 us -> 14.7 us
    unnamed x9 -> x2, waiting for transfers between devices: 132 us -> 0.03 us
    pallas_call x0 -> x1, Pallas kernels: none -> 94.5 us  [forward(): pl.pallas_call(forward_kernel, out_shape=(jax.ShapeDtypeStruct((8, 256, 1...]
    all_to_all x2 -> x0, blocking collectives: 90 us -> none  [the longest x1 58 us: per_device(): lax.all_to_all(view_rows, 'dp', split_axis=2, concat_axis=1, tiled=True)]
    psum x4 -> x2, blocking collectives: 198 us -> 127 us  [the longest x1 64.5 us: per_device(): lax.psum((jnp.sum(weight * weight), jnp.sum(wg * wg)), ('dp', 'feat'))]
    all_gather x4 -> x2, waiting for transfers between devices: 200 us -> 150 us  [the longest x1 77.4 us: per_device(): lax.all_gather(half, 'dp', axis=1, tiled=True, axis_index_groups=group)]
    reduce_scatter x1 -> x0, waiting for transfers between devices: 39.2 us -> none  [per_device(): lax.psum_scatter(exchanged, 'feat', scatter_dimension=1, tiled=True)]
    unnamed x16 -> x8, local copies, waits for them, and re-layouts: 27.7 us -> 1.21 us
    dot_general x5 -> x3, matrix products: 36.8 us -> 14.7 us  [the longest x1 7.58 us: per_device(): lax.dot_general(xg.reshape(2048, 1024), og, (((0,), (0,)), ((), ())), pre...]
  transfers between devices with their start and end apart: 8 -> 6, of which waited for: 8 -> 5; matrix products, arithmetic and copies ran while one was open for 2% -> 1% of each run, Pallas kernels for 0% -> 0%
where the time goes in v1:
time: 454 us
  waiting for transfers between devices  167 us (37%)
  blocking collectives  127 us (28%)
  Pallas kernels  94.5 us (21%)
  starting transfers between devices  19 us (4%)
  between operations  15.6 us (3%)
  matrix products  14.7 us (3%)
  other arithmetic  12.3 us (3%)
    pallas_call x1, Pallas kernels, forward(): pl.pallas_call(forward_kernel, out_shape=(jax.ShapeDtypeStruct((8, 256, 1...  94.5 us
    all_gather x1, waiting for transfers between devices, per_device(): lax.all_gather(half, 'dp', axis=1, tiled=True, axis_index_groups=group)  77.4 us
    all_gather x1, waiting for transfers between devices, per_device(): og = lax.all_gather(og, 'dp', axis=1, tiled=True, axis_index_groups=group)  72.4 us
    psum x1, blocking collectives, per_device(): lax.psum((jnp.sum(weight * weight), jnp.sum(wg * wg)), ('dp', 'feat'))  64.5 us
    psum x1, blocking collectives, per_device(): gram = lax.psum(part.astype(F32), 'feat').astype(BF)  62.4 us
    ppermute x1, starting transfers between devices, per_device(): gram = lax.ppermute(gram, 'dp', swap)  11 us
    all_to_all x1, waiting for transfers between devices, per_device(): lax.all_to_all(grads, 'dp', 1, 0, tiled=True, axis_index_groups=group)  10.7 us
  transfers between devices with their start and end apart: 6, of which 5 were waited for; matrix products, arithmetic and copies ran while one was open for 1% of the time, Pallas kernels for 0%

profile of v1, /device:TPU:1, one launch (start us, length us, event | category | flops | bytes accessed | tf_op | source)
XLA Modules:
  0.0 454.0 jit_solution(3485890398145426517)
XLA Ops:
  7.2 94.5 %shard_map.50 = (bf16[8,256,1024]{2,1,0:T(8,128)(2,1)}, f32[2048,128]{1,0:T(8,128)}, bf16[2048,128]{1,0:T(8,128)(2,1)}, f32[8,128]{1,0:T(8,128)}) custom-call(bf16[2,128,1024]{2,1,0:T(8,128)(2,1)} %x_ref.1, f32[512,1024]{1,0:T(8,128)} %w_ref.1), custom_call_target="tpu_custom_call" | custom-call | tf_op jit(solution)/shard_map/pallas_call | solution.py:246
  101.7 77.4 %all-gather.3.cloned.1.call-done = bf16[2048,1024]{1,0:T(8,128)(2,1)} async-done(((bf16[2048,128]{1,0:T(8,128)(2,1)}), bf16[2048,1024]{1,0:T(8,128)(2,1)}) %all-gather.3.cloned.1.call-update) | async-done | bytes 4194320 | tf_op jit(solution)/shard_map/all_gather | solution.py:280
  179.1 3.6 fusion
  182.8 62.4 %all-reduce.2 = bf16[256,2048]{1,0:T(8,128)(2,1)} all-reduce(f32[256,2048]{1,0:T(8,128)S(1)} %fusion), channel_id=1, replica_groups=mesh['dp'=16,'feat'=8] {'feat'}, use_global_device_ids=true, to_apply=%region_2.3 | all-reduce | flops 524288 | bytes 3145728 | tf_op jit(solution)/shard_map/psum | solution.py:283
  245.2 11.0 %collective-permute-start = (bf16[256,2048]{1,0:T(8,128)(2,1)}, bf16[256,2048]{1,0:T(8,128)(2,1)S(1)}, u32[]{:S(2)}, u32[]{:S(2)}) collective-permute-start(bf16[256,2048]{1,0:T(8,128)(2,1)} %all-reduce.2), channel_id=1, source_target_pairs={{0,8},{8,0},{16,24},{24,16},{32,40},{40,32},{48,56},{56,48},{64,72... | collective-permute-start | bytes 3145736 | tf_op jit(solution)/shard_map/ppermute | solution.py:284
  256.2 3.2 collective-permute-done
  259.4 3.5 fusion.2
  262.9 0.9 copy.8
  263.8 6.4 %all-to-all-start = ((bf16[256,8,128]{2,0,1:T(8,128)(2,1)}), bf16[256,8,128]{2,0,1:T(8,128)(2,1)S(1)}, u32[]{:S(2)}, u32[]{:S(2)}) async-start(bf16[256,8,128]{2,0,1:T(8,128)(2,1)} %bitcast.22), calls=%async_computation | async-start | bytes 1048576 | tf_op jit(solution)/shard_map/all_to_all | solution.py:287
  270.2 0.7 slice_bitcast_fusion
  270.9 0.3 fusion.3
  271.2 10.7 %all-to-all-done = bf16[256,8,128]{2,0,1:T(8,128)(2,1)S(1)} async-done(((bf16[256,8,128]{2,0,1:T(8,128)(2,1)}), bf16[256,8,128]{2,0,1:T(8,128)(2,1)S(1)}, u32[]{:S(2)}, u32[]{:S(2)}) %all-to-all-start) | async-done | bytes 524320 | tf_op jit(solution)/shard_map/all_to_all | solution.py:287
  281.9 0.3 fusion.6
  282.2 1.1 multiply_convert_fusion
  283.4 72.4 %all-gather.5.cloned.1.call-done = bf16[2048,1024]{1,0:T(8,128)(2,1)} async-done(((bf16[2048,128]{1,0:T(8,128)(2,1)}), bf16[2048,1024]{1,0:T(8,128)(2,1)}) %all-gather.5.cloned.1.call-update) | async-done | bytes 4194320 | tf_op jit(solution)/shard_map/all_gather | solution.py:294
  355.7 7.6 %fusion.8 = f32[1024,1024]{1,0:T(8,128)S(1)} fusion(bf16[2048,1024]{1,0:T(8,128)(2,1)} %bitcast.23, bf16[2048,1024]{1,0:T(8,128)(2,1)} %all-gather.5.cloned.1.call-done), kind=kOutput, calls=%fused_computation.25 | convolution fusion | flops 4294967296 | bytes 12582912 | tf_op jit(solution)/shard_map/dot_general | solution.py:295
  363.3 1.6 constant_dynamic-slice_fusion
  364.9 1.2 copy-done.1
  366.1 1.5 collective-permute-start.2
  367.7 1.1 multiply_reduce_fusion.1
  368.8 3.0 collective-permute-done.2
  371.8 3.4 multiply_reduce_fusion
  375.2 64.5 %all-reduce = (f32[]{:T(128)}, f32[]{:T(128)}) all-reduce(f32[]{:T(128)} %multiply_reduce_fusion.1, f32[]{:T(128)} %multiply_reduce_fusion), channel_id=1, replica_groups=mesh['dp'=16,'feat'=8] {'dp','feat'}, use_global_device_ids=true, to_apply=%region_1.2 | all-reduce | flops 2 | bytes 16 | tf_op jit(solution)/shard_map/psum | solution.py:299
  441.0 6.1 %multiply_subtract_fusion = (f32[512,1024]{1,0:T(8,128)}, f32[512,1024]{1,0:T(8,128)}) fusion(f32[512,1024]{1,0:T(8,128)S(1)} %copy-done, f32[512,1024]{1,0:T(8,128)} %collective-permute-done.2, f32[1024,1024]{1,0:T(8,128)} %copy-done.1, s32[]{:T(128)S(6)} %select_n.23, f32[]{:T(128)S(6)} %div.30, f32[512,1024]{1,0:T(8,128)} %param.5), kind=kLoop, calls=%fused_computation.2 | loop fusion | flops 3145728 | bytes 12582920 | tf_op jit(solution)/shard_map/sub | solution.py:302
  (15 shorter events, 0.1 us)
Async XLA Ops:
  7.2 171.9 %all-gather.3.cloned.1.call-start = ((), (), s32[]{:S(2)}) async-start(), calls=%async_computation.1 | async-start | bytes 4718592 | tf_op jit(solution)/shard_map/all_gather | solution.py:280
  182.8 73.4 %copy-start.3 = (bf16[2048,128]{1,0:T(8,128)(2,1)S(1)}, bf16[2048,128]{1,0:T(8,128)(2,1)}, u32[]{:S(2)}) copy-start(bf16[2048,128]{1,0:T(8,128)(2,1)} %get-tuple-element.8) | copy-start | bytes 1572868
  245.2 14.3 %collective-permute-start = (bf16[256,2048]{1,0:T(8,128)(2,1)}, bf16[256,2048]{1,0:T(8,128)(2,1)S(1)}, u32[]{:S(2)}, u32[]{:S(2)}) collective-permute-start(bf16[256,2048]{1,0:T(8,128)(2,1)} %all-reduce.2), channel_id=1, source_target_pairs={{0,8},{8,0},{16,24},{24,16},{32,40},{40,32},{48,56},{56,48},{64,72... | collective-permute-start | bytes 3145736 | tf_op jit(solution)/shard_map/ppermute | solution.py:284
  256.2 14.7 %collective-permute-start.1 = (bf16[2048,128]{1,0:T(8,128)(2,1)S(1)}, bf16[2048,128]{1,0:T(8,128)(2,1)S(1)}, u32[]{:S(2)}, u32[]{:S(2)}) collective-permute-start(bf16[2048,128]{1,0:T(8,128)(2,1)S(1)} %copy-done.3), channel_id=1, source_target_pairs={{0,8},{8,0},{16,24},{24,16},{32,40},{40,32},{48,56},{56,48},{64,72... | collective-permute-start | bytes 1572872 | tf_op jit(solution)/shard_map/ppermute | solution.py:278
  262.9 19.1 %copy-start.2 = (f32[2048,128]{1,0:T(8,128)S(1)}, f32[2048,128]{1,0:T(8,128)}, u32[]{:S(2)}) copy-start(f32[2048,128]{1,0:T(8,128)} %get-tuple-element.9) | copy-start | bytes 3145732
  263.8 18.2 %all-to-all-start = ((bf16[256,8,128]{2,0,1:T(8,128)(2,1)}), bf16[256,8,128]{2,0,1:T(8,128)(2,1)S(1)}, u32[]{:S(2)}, u32[]{:S(2)}) async-start(bf16[256,8,128]{2,0,1:T(8,128)(2,1)} %bitcast.22), calls=%async_computation | async-start | bytes 1048576 | tf_op jit(solution)/shard_map/all_to_all | solution.py:287
  270.2 85.5 %all-gather.5.cloned.1.call-start = ((), (), s32[]{:S(2)}) async-start(), calls=%async_computation.2 | async-start | bytes 4718592 | tf_op jit(solution)/shard_map/all_gather | solution.py:294
  363.3 2.8 copy-start.1
  363.3 4.3 copy-start
  366.1 5.7 %collective-permute-start.2 = (f32[512,1024]{1,0:T(8,128)}, f32[512,1024]{1,0:T(8,128)}, u32[]{:S(2)}, u32[]{:S(2)}) collective-permute-start(f32[512,1024]{1,0:T(8,128)} %constant_dynamic-slice_fusion), channel_id=1, source_target_pairs={{0,8},{8,0},{16,24},{24,16},{32,40},{40,32},{48,56},{56,48},{64,72... | collective-permute-start | bytes 6291464 | tf_op jit(solution)/shard_map/ppermute | solution.py:298
Sparse Core Ops, SparseCore 0:
  101.8 77.2 all-gather.2
  283.5 72.2 all-gather.4

commit v2 on v1

--- a/solution.py
+++ b/solution.py
@@ -47,7 +47,7 @@
 
 
 class Gather:
-    def __init__(self, q, r, device, piece, send, recv):
+    def __init__(self, q, r, device, piece, send, recv, count=NCH):
         up, down, far, other = (r + 1) % 4, (r + 3) % 4, (r + 2) % 4, 1 - q
         self.blocks = [
             other * 4 + r, q * 4 + down, q * 4 + up, q * 4 + far,
@@ -61,7 +61,7 @@
 
         to_up, to_down, to_pair = device(q, up), device(q, down), device(other, r)
         self.copies = []
-        for k in range(NCH):
+        for k in range(count):
             self.copies.append([
                 make(mine, k, 0, to_pair),
                 make(mine, k, 1, to_up),
@@ -269,36 +269,217 @@
     )(view_features, weight)
 
 
+def aligned(i, size):
+    return pl.ds(pl.multiple_of(i * size, size), size)
+
+
+def backward_kernel(
+    xg, normed_ref, half_ref, inv_ref, w_ref, wg_ref, trust_ref,
+    hg, hother, gs, gr, zs, zr, gram, ts, tr, og, wacc, wrecv, msg, got, mid, got2,
+    c_s, c_r, h_s, h_r, g_s, g_r, z_s, z_r, gg_s, gg_r, t_s, t_r, o_s, o_r, w_s, w_r, n_s, n_r, m_s, m_r,
+):
+    me = Place()
+    d, p, f, c, x, y, zh, zl = me.d, me.p, me.f, me.c, me.x, me.y, me.zh, me.zl
+    n = 2048
+    partners = [((d + i) % 16, f) for i in range(1, 16)]
+    partners += [(d, (f + i) % 8) for i in range(1, 8)]
+    partners += [me.at(c=1 - c, y=(y + i) % 4) for i in range(1, 4)]
+    for t in partners:
+        signal(t)
+    hg[:, aligned(p, 128)] = half_ref[...]
+    pl.semaphore_wait(pltpu.get_barrier_semaphore(), len(partners))
+
+    def over_dp(q, r):
+        return me.at(zh=q, x=r)
+
+    ag = Gather(zh, x, over_dp, lambda b, k: hg.at[pl.ds(k * 512, 512), aligned(b, 128)], h_s, h_r)
+    for k in range(NCH):
+        ag.own(k)
+    swap = remote(half_ref, hother, c_s, c_r, me.at(c=1 - c))
+    swap.start()
+    squares = jnp.sum(w_ref[...] * w_ref[...], 0, keepdims=True)
+    for k in range(NCH):
+        ag.near(k)
+    for k in range(NCH):
+        ag.far(k)
+    for k in range(NCH):
+        for slot in (4, 5, 6):
+            ag.rest(k, slot)
+
+    gcopies = []
+    for dy in (2, 1, 3, 0):
+        yt = (y + dy) % 4
+        for side in range(2):
+            gs[yt, side] = lax.dot_general(
+                hg[aligned(p, 256), :], hg[aligned(side * 4 + yt, 256), :],
+                (((1,), (1,)), ((), ())), preferred_element_type=F32,
+            ).astype(BF)
+        copy = remote(gs.at[yt], gr.at[dy], g_s.at[dy], g_r.at[dy], me.at(c=1 - c, y=yt))
+        copy.start()
+        gcopies.append(copy)
+    swap.wait_recv()
+    corr = jnp.sum(half_ref[...].astype(F32) * hother[...].astype(F32), 0, keepdims=True) / n
+    extra = (-2.0 * (1.0 - corr) - 2.0 * REDUNDANCY * corr) / n
+    for copy in gcopies:
+        copy.wait_recv()
+
+    def total(side):
+        s = gr[0, side].astype(F32)
+        for i in range(1, 4):
+            s = s + gr[i, side].astype(F32)
+        return s
+
+    zs[...] = total(1 - zl).astype(BF)
+    zcopy = remote(zs, zr, z_s, z_r, me.at(zl=1 - zl))
+    zcopy.start()
+    keep = total(zl)
+    zcopy.wait_recv()
+    gram[:, aligned(f, 256)] = (keep + zr[...].astype(F32)).astype(BF)
+    gg = Gather(
+        zl, y, lambda q, r: me.at(zl=q, y=r),
+        lambda b, k: gram.at[pl.ds(k * 128, 128), aligned(b, 256)], gg_s, gg_r, 2,
+    )
+    for k in range(2):
+        gg.own(k)
+    for k in range(2):
+        gg.near(k)
+    for k in range(2):
+        gg.far(k)
+    for k in range(2):
+        for slot in (4, 5, 6):
+            gg.rest(k, slot)
+
+    kappa = 2.0 * REDUNDANCY / (n * n)
+    for j in range(4):
+        part = kappa * jnp.dot(gram[...], hg[:, pl.ds(j * 256, 256)], preferred_element_type=F32)
+        ts[2 * j] = part[:, :128].astype(BF)
+        ts[2 * j + 1] = part[:, 128:].astype(BF)
+    tcopies = []
+    for i in (2, 6, 5, 4, 3, 1, 7):
+        pt = (p + i) % 8
+        copy = remote(
+            ts.at[pt], tr.at[aligned(p, 256)], t_s.at[i - 1], t_r.at[i - 1], (pt * 2 + c, f)
+        )
+        copy.start()
+        tcopies.append(copy)
+    tr[aligned(p, 256), :] = ts[p]
+    for copy in tcopies:
+        copy.wait_recv()
+    grads = tr[...].astype(F32) + extra * hother[...].astype(F32)
+    normed = normed_ref[...]
+    mean = jnp.sum(grads, 0, keepdims=True) / n
+    cross = jnp.sum(grads * normed, 0, keepdims=True) / n
+    og[:, aligned(p, 128)] = (inv_ref[0:1, :] * (grads - mean - normed * cross)).astype(BF)
+
+    oo = Gather(zh, x, over_dp, lambda b, k: og.at[pl.ds(k * 512, 512), aligned(b, 128)], o_s, o_r)
+    for k in range(NCH):
+        oo.own(k)
+    for k in range(NCH):
+        oo.near(k)
+    for k in range(NCH):
+        oo.far(k)
+    wcopy = remote(wacc.at[aligned(1 - c, 512)], wrecv, w_s, w_r, me.at(c=1 - c))
+    for k in range(NCH):
+        for slot in (4, 5, 6):
+            oo.rest(k, slot)
+        rows = pl.ds(k * 512, 512)
+        for side in range(2):
+            core = (1 - c) if side == 0 else c
+
+            @pl.loop(0, 2)
+            def _(m):
+                cols = aligned(core * 2 + m, 256)
+                part = lax.dot_general(
+                    xg[rows, cols], og[rows, :], (((0,), (0,)), ((), ())), preferred_element_type=F32
+                )
+                if k == 0:
+                    wacc[cols, :] = part
+                else:
+                    wacc[cols, :] += part
+
+            if k == NCH - 1 and side == 0:
+                wcopy.start()
+    wcopy.wait_recv()
+    wg = wacc[aligned(c, 512), :] + wrecv[...]
+    wg_ref[...] = wg
+    grad_squares = jnp.sum(wg * wg, 0, keepdims=True)
+
+    def fold(v):
+        s = v[:, :128]
+        for i in range(1, 8):
+            s = s + v[:, i * 128:(i + 1) * 128]
+        return s
+
+    msg[...] = jnp.zeros_like(msg)
+    msg[0:1, :] = fold(grad_squares)
+    msg[1:2, :] = fold(squares)
+    ncopies = []
+    for i in range(1, 16):
+        copy = remote(msg, got.at[i - 1], n_s.at[i - 1], n_r.at[i - 1], ((d + i) % 16, f))
+        copy.start()
+        ncopies.append(copy)
+    s = msg[...]
+    for i, copy in enumerate(ncopies):
+        copy.wait_recv()
+        s = s + got[i]
+    mid[...] = s
+    mcopies = []
+    for i in range(1, 8):
+        copy = remote(mid, got2.at[i - 1], m_s.at[i - 1], m_r.at[i - 1], (d, (f + i) % 8))
+        copy.start()
+        mcopies.append(copy)
+    for i, copy in enumerate(mcopies):
+        copy.wait_recv()
+        s = s + got2[i]
+    sums = jnp.sqrt(jnp.sum(s, 1, keepdims=True))
+    trust_ref[...] = jnp.broadcast_to(sums[1:2, :] / (sums[0:1, :] + NORM_EPSILON), (8, 128))
+    for copy in [swap, zcopy, wcopy] + gcopies + tcopies + ncopies + mcopies:
+        copy.wait_send()
+    for g in (ag, gg, oo):
+        g.close()
+
+
+def backward(xg, normed, half, inverse, weight):
+    dma = pltpu.SemaphoreType.DMA
+    return pl.pallas_call(
+        backward_kernel,
+        out_shape=(
+            jax.ShapeDtypeStruct((512, 1024), F32),
+            jax.ShapeDtypeStruct((8, 128), F32),
+        ),
+        in_specs=vmem(5),
+        out_specs=tuple(vmem(2)),
+        scratch_shapes=[
+            pltpu.VMEM((2048, 1024), BF),
+            pltpu.VMEM((2048, 128), BF),
+            pltpu.VMEM((4, 2, 256, 256), BF),
+            pltpu.VMEM((4, 2, 256, 256), BF),
+            pltpu.VMEM((256, 256), BF),
+            pltpu.VMEM((256, 256), BF),
+            pltpu.VMEM((256, 2048), BF),
+            pltpu.VMEM((8, 256, 128), BF),
+            pltpu.VMEM((2048, 128), BF),
+            pltpu.VMEM((2048, 1024), BF),
+            pltpu.VMEM((1024, 1024), F32),
+            pltpu.VMEM((512, 1024), F32),
+            pltpu.VMEM((8, 128), F32),
+            pltpu.VMEM((15, 8, 128), F32),
+            pltpu.VMEM((8, 128), F32),
+            pltpu.VMEM((7, 8, 128), F32),
+            dma, dma, dma((7, NCH)), dma((7, NCH)), dma((4,)), dma((4,)), dma, dma,
+            dma((7, 2)), dma((7, 2)), dma((7,)), dma((7,)), dma((7, NCH)), dma((7, NCH)),
+            dma, dma, dma((15,)), dma((15,)), dma((7,)), dma((7,)),
+        ],
+        compiler_params=pltpu.CompilerParams(
+            collective_id=1, has_side_effects=True, vmem_limit_bytes=60 * 2**20
+        ),
+    )(xg.reshape(2048, 1024), normed, half, inverse, weight)
+
+
 def per_device(view_features, weight, velocity):
-    d, f = lax.axis_index("dp"), lax.axis_index("feat")
-    p, c = d // 2, d % 2
     xg, normed, half, inverse = forward(view_features, weight)
-    swap = [(i, i ^ 1) for i in range(16)]
-    group = [[q * 2 + k for q in range(8)] for k in range(2)]
-    other = lax.ppermute(half, "dp", swap)
-    n = 2048
-    wide = lax.all_gather(half, "dp", axis=1, tiled=True, axis_index_groups=group)
-    mine = lax.dynamic_slice_in_dim(wide, p * 256, 256, 0)
-    part = lax.dot_general(mine, wide, (((1,), (1,)), ((), ())), preferred_element_type=F32).astype(BF)
-    gram = lax.psum(part.astype(F32), "feat").astype(BF)
-    gram = lax.ppermute(gram, "dp", swap)
-    kappa = 2.0 * REDUNDANCY / (n * n)
-    grads = (kappa * jnp.dot(gram, wide, preferred_element_type=F32)).astype(BF)
-    grads = lax.all_to_all(grads, "dp", 1, 0, tiled=True, axis_index_groups=group).astype(F32)
-    corr = jnp.sum(half.astype(F32) * other.astype(F32), 0) / n
-    extra = (-2.0 * (1.0 - corr) - 2.0 * REDUNDANCY * corr) / n
-    grads = grads + extra * other.astype(F32)
-    mean = jnp.mean(grads, 0)
-    cross = jnp.mean(grads * normed, 0)
-    og = (inverse[0] * (grads - mean - normed * cross)).astype(BF)
-    og = lax.all_gather(og, "dp", axis=1, tiled=True, axis_index_groups=group)
-    wg = lax.dot_general(xg.reshape(2048, 1024), og, (((0,), (0,)), ((), ())), preferred_element_type=F32)
-    keep = lax.dynamic_slice_in_dim(wg, c * 512, 512, 0)
-    give = lax.dynamic_slice_in_dim(wg, (1 - c) * 512, 512, 0)
-    wg = keep + lax.ppermute(give, "dp", swap)
-    wsq, gsq = lax.psum((jnp.sum(weight * weight), jnp.sum(wg * wg)), ("dp", "feat"))
-    trust = jnp.sqrt(wsq) / (jnp.sqrt(gsq) + NORM_EPSILON)
-    new_velocity = MOMENTUM * velocity + trust * wg
+    wg, trust = backward(xg, normed, half, inverse, weight)
+    new_velocity = MOMENTUM * velocity + trust[0:1, 0:1] * wg
     return weight - LEARN_RATE * new_velocity, new_velocity
 
 

time: 454 us -> 237 us (0.52)
  waiting for transfers between devices: 167 us -> 0 us
  Pallas kernels: 94.5 us -> 229 us
  blocking collectives: 127 us -> 0 us
  starting transfers between devices: 19 us -> 0 us
  between operations: 15.6 us -> 0.65 us
  matrix products: 14.7 us -> 0 us
  other arithmetic: 12.3 us -> 6.07 us
    all_gather x2 -> x0, waiting for transfers between devices: 150 us -> none  [the longest x1 77.4 us: per_device(): lax.all_gather(half, 'dp', axis=1, tiled=True, axis_index_groups=group)]
    pallas_call x0 -> x1, Pallas kernels: none -> 135 us  [backward(): pl.pallas_call(backward_kernel, out_shape=(jax.ShapeDtypeStruct((512, 102...]
    psum x2 -> x0, blocking collectives: 127 us -> none  [the longest x1 64.5 us: per_device(): lax.psum((jnp.sum(weight * weight), jnp.sum(wg * wg)), ('dp', 'feat'))]
    dot_general x3 -> x0, matrix products: 14.7 us -> none  [the longest x1 7.58 us: per_device(): lax.dot_general(xg.reshape(2048, 1024), og, (((0,), (0,)), ((), ())), pre...]
    ppermute x3 -> x0, starting transfers between devices: 12.6 us -> none  [the longest x1 11 us: per_device(): gram = lax.ppermute(gram, 'dp', swap)]
    all_to_all x1 -> x0, waiting for transfers between devices: 10.7 us -> none  [per_device(): lax.all_to_all(grads, 'dp', 1, 0, tiled=True, axis_index_groups=group)]
    all_to_all x1 -> x0, starting transfers between devices: 6.42 us -> none  [per_device(): lax.all_to_all(grads, 'dp', 1, 0, tiled=True, axis_index_groups=group)]
    ppermute x3 -> x0, waiting for transfers between devices: 6.23 us -> none  [the longest x1 3.24 us: per_device(): gram = lax.ppermute(gram, 'dp', swap)]
  transfers between devices with their start and end apart: 6 -> 0, of which waited for: 5 -> 0; matrix products, arithmetic and copies ran while one was open for 1% -> 0% of each run, Pallas kernels for 0% -> 0%
where the time goes in v2:
time: 237 us
  Pallas kernels  229 us (97%)
  other arithmetic  6.07 us (3%)
    pallas_call x1, Pallas kernels, backward(): pl.pallas_call(backward_kernel, out_shape=(jax.ShapeDtypeStruct((512, 102...  135 us
    pallas_call x1, Pallas kernels, forward(): pl.pallas_call(forward_kernel, out_shape=(jax.ShapeDtypeStruct((8, 256, 1...  94.5 us
    sub x1, other arithmetic, per_device(): return (weight - LEARN_RATE * new_velocity, new_velocity)  6.07 us

profile of v2, /device:TPU:1, one launch (start us, length us, event | category | flops | bytes accessed | tf_op | source)
XLA Modules:
  0.0 236.9 jit_solution(13316508585672325333)
XLA Ops:
  0.6 94.5 %shard_map.50 = (bf16[8,256,1024]{2,1,0:T(8,128)(2,1)}, f32[2048,128]{1,0:T(8,128)}, bf16[2048,128]{1,0:T(8,128)(2,1)}, f32[8,128]{1,0:T(8,128)}) custom-call(bf16[2,128,1024]{2,1,0:T(8,128)(2,1)} %x_ref.1, f32[512,1024]{1,0:T(8,128)} %w_ref.3), custom_call_target="tpu_custom_call" | custom-call | tf_op jit(solution)/shard_map/pallas_call | solution.py:246
  95.1 0.0 copy-start
  95.1 134.5 %shard_map.51 = (f32[512,1024]{1,0:T(8,128)}, f32[8,128]{1,0:T(8,128)}) custom-call(bf16[2048,1024]{1,0:T(8,128)(2,1)} %bitcast.2, f32[2048,128]{1,0:T(8,128)} %get-tuple-element.9.normed_ref, bf16[2048,128]{1,0:T(8,128)(2,1)} %get-tuple-element.10.half_ref, f32[8,128]{1,0:T(8,128)} %get-tuple-element.11.inv_ref, f32[512,1024]{1,0:T(8,128)} %w_ref.3), custom_call_target="tpu_custom_call" | custom-call | tf_op jit(solution)/shard_map/pallas_call | solution.py:444
  229.7 1.2 slice.3
  230.9 0.0 copy-done
  230.9 6.1 %multiply_subtract_fusion = (f32[512,1024]{1,0:T(8,128)}, f32[512,1024]{1,0:T(8,128)}) fusion(f32[512,1024]{1,0:T(8,128)S(1)} %copy-done, f32[512,1024]{1,0:T(8,128)} %get-tuple-element.13, f32[]{:T(128)} %bitcast.1, f32[512,1024]{1,0:T(8,128)} %param.5), kind=kLoop, calls=%fused_computation | loop fusion | flops 2621440 | bytes 10485764 | tf_op jit(solution)/shard_map/sub | solution.py:483
Async XLA Ops:
  95.1 135.8 %copy-start = (f32[512,1024]{1,0:T(8,128)S(1)}, f32[512,1024]{1,0:T(8,128)}, u32[]{:S(2)}) copy-start(f32[512,1024]{1,0:T(8,128)} %w_ref.3) | copy-start | bytes 6291460

commit v3 on v2

v3 whole, which is shorter than its diff:
```python
import functools

import jax
import jax.numpy as jnp
from jax import lax
from jax.experimental import pallas as pl
from jax.experimental.pallas import tpu as pltpu
from jax.sharding import PartitionSpec as P

EPSILON = 1e-05
NORM_EPSILON = 1e-06
REDUNDANCY = 0.0051
MOMENTUM = 0.9
LEARN_RATE = 0.2
MESH = pl.DeviceIdType.MESH
BF = jnp.bfloat16
F32 = jnp.float32
NCH = 4


class Place:
    def __init__(self):
        d, f = lax.axis_index("dp"), lax.axis_index("feat")
        self.d, self.f, self.p = d, f, d // 2
        self.zh, self.x, self.c = d // 8, (d // 2) % 4, d % 2
        self.zl, self.y = f // 4, f % 4

    def at(self, zh=None, x=None, c=None, zl=None, y=None):
        zh = self.zh if zh is None else zh
        x = self.x if x is None else x
        c = self.c if c is None else c
        zl = self.zl if zl is None else zl
        y = self.y if y is None else y
        return ((zh * 4 + x) * 2 + c, zl * 4 + y)

    def along(self, i):
        zero = self.c == 0
        return (jnp.where(zero, i * 2, self.d), jnp.where(zero, self.f, i))

    def across(self, i):
        zero = self.c == 0
        return (jnp.where(zero, self.d, i * 2 + 1), jnp.where(zero, i, self.f))

    def across_swapped(self, i):
        zero = self.c == 0
        return (jnp.where(zero, self.d + 1, i * 2), jnp.where(zero, i, self.f))


def signal(target):
    pl.semaphore_signal(
        pltpu.get_barrier_semaphore(), inc=1, device_id=target, device_id_type=MESH
    )


def remote(src, dst, send, recv, target):
    return pltpu.make_async_remote_copy(
        src_ref=src, dst_ref=dst, send_sem=send, recv_sem=recv, device_id=target, device_id_type=MESH
    )


class Gather:
    def __init__(self, q, r, device, piece, send, recv, count=NCH, paired=range(NCH)):
        up, down, far, other = (r + 1) % 4, (r + 3) % 4, (r + 2) % 4, 1 - q
        self.blocks = [
            other * 4 + r, q * 4 + down, q * 4 + up, q * 4 + far,
            other * 4 + down, other * 4 + up, other * 4 + far,
        ]
        mine = q * 4 + r
        self.paired = paired
        self.count = count

        def make(block, k, slot, target):
            ref = piece(block, k)
            return remote(ref, ref, send.at[slot, k], recv.at[slot, k], target)

        to_up, to_down, to_pair = device(q, up), device(q, down), device(other, r)
        self.copies = []
        for k in range(count):
            if k in paired:
                last = make(self.blocks[3], k, 6, to_pair)
            elif k % 2 == 0:
                last = make(self.blocks[4], k, 6, to_up)
            else:
                last = make(self.blocks[5], k, 6, to_down)
            self.copies.append([
                make(mine, k, 0, to_pair),
                make(mine, k, 1, to_up),
                make(mine, k, 2, to_down),
                make(self.blocks[1], k, 3, to_up) if k % 2 == 0 else make(self.blocks[2], k, 3, to_down),
                make(self.blocks[0], k, 4, to_up),
                make(self.blocks[0], k, 5, to_down),
                last,
            ])

    def own(self, k):
        for slot in (0, 1, 2):
            self.copies[k][slot].start()

    def near(self, k):
        c = self.copies[k]
        first = 1 + k % 2
        c[first].wait_recv()
        c[3].start()
        c[0].wait_recv()
        c[4].start()
        c[5].start()
        c[3 - first].wait_recv()

    def far(self, k):
        c = self.copies[k]
        if k in self.paired:
            c[3].wait_recv()
            c[6].start()

    def rest(self, k):
        c = self.copies[k]
        if k not in self.paired:
            c[4 + k % 2].wait_recv()
            c[6].start()
            c[3].wait_recv()
            c[5 - k % 2].wait_recv()
        else:
            c[4].wait_recv()
            c[5].wait_recv()

    def last(self, k):
        self.copies[k][6].wait_recv()

    def run(self):
        for step in (self.own, self.near, self.far, self.rest, self.last):
            for k in range(self.count):
                step(k)

    def close(self):
        for c in self.copies:
            for copy in c:
                copy.wait_send()


def aligned(i, size):
    return pl.ds(pl.multiple_of(i * size, size), size)


def kernel(
    x_ref, w_ref, wg_ref, trust_ref,
    st, xg, wf, ys, yr, zs, zr, yacc, normed_ref, half_ref,
    hg, hother, gs, gr, gzs, gzr, gram, ts, tr, og, wacc, wrecv, msg, got, mid, got2,
    p1_s, p1_r, p2_s, p2_r, v_s, v_r, ag_s, ag_r, rs_s, rs_r, z_s, z_r,
    c_s, c_r, h_s, h_r, g_s, g_r, gz_s, gz_r, gg_s, gg_r, t_s, t_r, o_s, o_r, w_s, w_r, n_s, n_r, m_s, m_r,
):
    me = Place()
    d, p, f, c, x, y, zh, zl = me.d, me.p, me.f, me.c, me.x, me.y, me.zh, me.zl
    n = 2048
    still = zh == zl
    partners = [((d + i) % 16, f) for i in range(1, 16)]
    partners += [(d, (f + i) % 8) for i in range(1, 8)]
    partners += [me.at(c=1 - c, y=(y + i) % 4) for i in range(1, 4)]
    partners += [me.at(zh=zl, x=(x + i) % 4, zl=zh) for i in range(1, 4)]
    mirror = me.at(zh=zl, zl=zh)
    for t in partners:
        signal(t)

    @pl.when(jnp.logical_not(still))
    def _():
        signal(mirror)

    pl.semaphore_wait(pltpu.get_barrier_semaphore(), len(partners) + jnp.where(still, 0, 1))

    phase1 = []
    for dj in (2, 1, 3, 0):
        for dv in (0, 1):
            v, j = (c + dv) % 2, (y + dj) % 4
            src = x_ref.at[v, aligned(j, 32)]
            dst = st.at[y, aligned(c, 32)]
            if dj == 0 and dv == 0:
                own = pltpu.make_async_copy(src, dst, p1_r.at[0, 0])
                own.start()
            else:
                copy = remote(src, dst, p1_s.at[dj, dv], p1_r.at[dj, dv], me.at(c=v, y=j))
                copy.start()
                phase1.append((dj, dv, copy))
    own_rows = aligned(c, 512)
    wf[own_rows, :] = w_ref[...].astype(BF)
    wcopy = remote(wf.at[own_rows], wf.at[own_rows], v_s, v_r, me.at(c=1 - c))
    wcopy.start()
    for dj, dv, copy in phase1:
        copy.wait_recv()
    own.wait()

    landing = pl.ds(pl.multiple_of((zh * 4 + y) * 256 + x * 64, 64), 64)
    phase2 = []
    for dx in (2, 1, 3, 0):
        xt = (x + dx) % 4
        phase2.append(remote(
            st.at[xt], xg.at[landing], p2_s.at[dx], p2_r.at[x], me.at(zh=zl, x=xt, zl=zh)
        ))
        if dx == 0:
            @pl.when(still)
            def _():
                pltpu.make_async_copy(st.at[x], xg.at[landing], p2_r.at[x]).start()

            @pl.when(jnp.logical_not(still))
            def _():
                phase2[-1].start()
        else:
            phase2[-1].start()

    ag = Gather(
        zl, y, lambda q, r: me.at(zl=q, y=r),
        lambda b, k: xg.at[pl.ds(pl.multiple_of(b * 256 + k * 64, 64), 64)], ag_s, ag_r,
    )
    for k in range(NCH):
        ref = xg.at[pl.ds(pl.multiple_of(f * 256 + k * 64, 64), 64)]
        pltpu.make_async_copy(ref, ref, p2_r.at[k]).wait()
        ag.own(k)
    wcopy.wait_recv()

    order = [f] + ag.blocks
    sends = []

    def product(o):
        rows = aligned(order[o], 256)

        @pl.loop(0, 4)
        def _(j):
            part = jnp.dot(xg[rows, :], wf[:, aligned(j, 256)], preferred_element_type=F32).astype(BF)
            ys[2 * (j % 2), j // 2, rows, :] = part[:, :128]
            ys[2 * (j % 2) + 1, j // 2, rows, :] = part[:, 128:]

        for dx in (2, 1, 3):
            xt = (x + dx) % 4
            copy = remote(
                ys.at[xt, :, rows], yr.at[dx - 1, :, rows], rs_s.at[dx - 1, o], rs_r.at[dx - 1, o], me.at(x=xt)
            )
            copy.start()
            sends.append(copy)

    product(0)
    for k in range(NCH):
        ag.near(k)
    product(1)
    product(2)
    product(3)
    for k in range(NCH):
        ag.far(k)
    product(4)
    for k in range(NCH):
        ag.rest(k)
    product(5)
    product(6)
    for k in range(NCH):
        ag.last(k)
    product(7)
    zcopies = []
    for o in range(8):
        rows = aligned(order[o], 256)
        for copy in sends[3 * o:3 * o + 3]:
            copy.wait_recv()

        def total(side):
            s = ys[x, side, rows, :].astype(F32)
            for i in range(3):
                s = s + yr[i, side, rows, :].astype(F32)
            return s

        zs[rows, :] = total(1 - zh).astype(BF)
        copy = remote(zs.at[rows], zr.at[rows], z_s.at[o], z_r.at[o], me.at(zh=1 - zh))
        copy.start()
        zcopies.append(copy)
        yacc[rows, :] = total(zh)
    for copy in zcopies:
        copy.wait_recv()
    outputs = yacc[...] + zr[...].astype(F32)
    average = jnp.sum(outputs, 0, keepdims=True) / n
    centered = outputs - average
    variance = jnp.sum(centered * centered, 0, keepdims=True) / n
    inverse = lax.rsqrt(variance + EPSILON)
    normed = centered * inverse
    normed_ref[...] = normed
    half_ref[...] = normed.astype(BF)

    mine, crossing = jnp.where(c == 0, p, f), jnp.where(c == 0, f, p)
    hg[:, aligned(mine, 128)] = normed.astype(BF)
    hh = Gather(
        mine // 4, mine % 4, lambda q, r: me.along(q * 4 + r),
        lambda b, k: hg.at[pl.ds(k * 512, 512), aligned(b, 128)], h_s, h_r, NCH, (1,),
    )
    for k in range(NCH):
        hh.own(k)
    swap = remote(half_ref, hother, c_s, c_r, me.at(c=1 - c))
    swap.start()
    squares = jnp.sum(w_ref[...] * w_ref[...], 0, keepdims=True)
    for step in (hh.near, hh.far, hh.rest, hh.last):
        for k in range(NCH):
            step(k)

    gcopies = []
    for i in (2, 1, 3, 0):
        t = (crossing + i) % 4
        for side in range(2):
            gs[t, side] = lax.dot_general(
                hg[aligned(side * 4 + t, 256), :], hg[aligned(mine, 256), :],
                (((1,), (1,)), ((), ())), preferred_element_type=F32,
            ).astype(BF)
        copy = remote(
            gs.at[t], gr.at[i], g_s.at[i], g_r.at[i], me.across_swapped((crossing // 4) * 4 + t)
        )
        copy.start()
        gcopies.append(copy)
    swap.wait_recv()
    corr = jnp.sum(half_ref[...].astype(F32) * hother[...].astype(F32), 0, keepdims=True) / n
    extra = (-2.0 * (1.0 - corr) - 2.0 * REDUNDANCY * corr) / n
    for copy in gcopies:
        copy.wait_recv()
    q = mine // 4

    def gram_total(side):
        s = gr[0, side].astype(F32)
        for i in range(1, 4):
            s = s + gr[i, side].astype(F32)
        return s

    gzs[...] = gram_total(1 - q).astype(BF)
    gzcopy = remote(gzs, gzr, gz_s, gz_r, me.along((1 - q) * 4 + mine % 4))
    gzcopy.start()
    keep = gram_total(q)
    gzcopy.wait_recv()
    gram[:, aligned(crossing, 256)] = (keep + gzr[...].astype(F32)).astype(BF)
    gg = Gather(
        crossing // 4, crossing % 4, lambda q, r: me.across(q * 4 + r),
        lambda b, k: gram.at[pl.ds(k * 128, 128), aligned(b, 256)], gg_s, gg_r, 2, (),
    )
    gg.run()

    kappa = 2.0 * REDUNDANCY / (n * n)
    for j in range(4):
        part = kappa * jnp.dot(gram[...], hg[:, pl.ds(j * 256, 256)], preferred_element_type=F32)
        ts[2 * j] = part[:, :128].astype(BF)
        ts[2 * j + 1] = part[:, 128:].astype(BF)
    tcopies = []
    for i in (2, 6, 5, 4, 3, 1, 7):
        to = (mine + i) % 8
        copy = remote(
            ts.at[to], tr.at[aligned(mine, 256)], t_s.at[i - 1], t_r.at[i - 1], me.along(to)
        )
        copy.start()
        tcopies.append(copy)
    tr[aligned(mine, 256), :] = ts[mine]
    for copy in tcopies:
        copy.wait_recv()
    grads = tr[...].astype(F32) + extra * hother[...].astype(F32)
    normed = normed_ref[...]
    mean = jnp.sum(grads, 0, keepdims=True) / n
    cross = jnp.sum(grads * normed, 0, keepdims=True) / n
    og[:, aligned(p, 128)] = (inverse * (grads - mean - normed * cross)).astype(BF)

    oo = Gather(
        zh, x, lambda q, r: me.at(zh=q, x=r),
        lambda b, k: og.at[pl.ds(k * 512, 512), aligned(b, 128)], o_s, o_r,
    )
    for step in (oo.own, oo.near, oo.far):
        for k in range(NCH):
            step(k)
    gcopy = remote(wacc.at[aligned(1 - c, 512)], wrecv, w_s, w_r, me.at(c=1 - c))
    for k in range(NCH):
        oo.rest(k)
        oo.last(k)
        rows = pl.ds(k * 512, 512)
        for side in range(2):
            core = (1 - c) if side == 0 else c

            @pl.loop(0, 2)
            def _(m):
                cols = aligned(core * 2 + m, 256)
                part = lax.dot_general(
                    xg[rows, cols], og[rows, :], (((0,), (0,)), ((), ())), preferred_element_type=F32
                )
                if k == 0:
                    wacc[cols, :] = part
                else:
                    wacc[cols, :] += part

            if k == NCH - 1 and side == 0:
                gcopy.start()
    gcopy.wait_recv()
    wg = wacc[aligned(c, 512), :] + wrecv[...]
    wg_ref[...] = wg
    grad_squares = jnp.sum(wg * wg, 0, keepdims=True)

    def fold(v):
        s = v[:, :128]
        for i in range(1, 8):
            s = s + v[:, i * 128:(i + 1) * 128]
        return s

    msg[...] = jnp.zeros_like(msg)
    msg[0:1, :] = fold(grad_squares)
    msg[1:2, :] = fold(squares)
    ncopies = []
    for i in range(1, 16):
        copy = remote(msg, got.at[i - 1], n_s.at[i - 1], n_r.at[i - 1], ((d + i) % 16, f))
        copy.start()
        ncopies.append(copy)
    s = msg[...]
    for i, copy in enumerate(ncopies):
        copy.wait_recv()
        s = s + got[i]
    mid[...] = s
    mcopies = []
    for i in range(1, 8):
        copy = remote(mid, got2.at[i - 1], m_s.at[i - 1], m_r.at[i - 1], (d, (f + i) % 8))
        copy.start()
        mcopies.append(copy)
    for i, copy in enumerate(mcopies):
        copy.wait_recv()
        s = s + got2[i]
    sums = jnp.sqrt(jnp.sum(s, 1, keepdims=True))
    trust_ref[...] = jnp.broadcast_to(sums[1:2, :] / (sums[0:1, :] + NORM_EPSILON), (8, 128))
    for copy in [swap, gzcopy, gcopy, wcopy] + sends + zcopies + gcopies + tcopies + ncopies + mcopies:
        copy.wait_send()
    for dj, dv, copy in phase1:
        copy.wait_send()
    for copy in phase2[:3]:
        copy.wait_send()

    @pl.when(jnp.logical_not(still))
    def _():
        phase2[3].wait_send()

    for g in (ag, hh, gg, oo):
        g.close()


def vmem(n):
    return [pl.BlockSpec(memory_space=pltpu.VMEM)] * n


def gradient(view_features, weight):
    dma = pltpu.SemaphoreType.DMA

    def v(*shape, kind=BF):
        return pltpu.VMEM(shape, kind)

    def two(*shape):
        return [dma(shape) if shape else dma] * 2

    return pl.pallas_call(
        kernel,
        out_shape=(
            jax.ShapeDtypeStruct((512, 1024), F32),
            jax.ShapeDtypeStruct((8, 128), F32),
        ),
        in_specs=vmem(2),
        out_specs=tuple(vmem(2)),
        scratch_shapes=[
            v(4, 64, 1024), v(2048, 1024), v(1024, 1024), v(4, 2, 2048, 128), v(3, 2, 2048, 128),
            v(2048, 128), v(2048, 128), v(2048, 128, kind=F32), v(2048, 128, kind=F32), v(2048, 128),
            v(2048, 1024), v(2048, 128), v(4, 2, 256, 256), v(4, 2, 256, 256), v(256, 256), v(256, 256),
            v(256, 2048), v(8, 256, 128), v(2048, 128), v(2048, 1024), v(1024, 1024, kind=F32),
            v(512, 1024, kind=F32), v(8, 128, kind=F32), v(15, 8, 128, kind=F32), v(8, 128, kind=F32),
            v(7, 8, 128, kind=F32),
            *two(4, 2), *two(4), *two(), *two(7, NCH), *two(3, 8), *two(8),
            *two(), *two(7, NCH), *two(4), *two(), *two(7, 2), *two(7), *two(7, NCH), *two(), *two(15), *two(7),
        ],
        compiler_params=pltpu.CompilerParams(
            collective_id=0, has_side_effects=True, vmem_limit_bytes=60 * 2**20
        ),
    )(view_features, weight)


def update_kernel(trust_ref, wg_ref, w_ref, v_ref, nw_ref, nv_ref):
    new_velocity = MOMENTUM * v_ref[...] + trust_ref[0:1, 0:1] * wg_ref[...]
    nv_ref[...] = new_velocity
    nw_ref[...] = w_ref[...] - LEARN_RATE * new_velocity


def update(trust, wg, weight, velocity):
    block = pl.BlockSpec((128, 1024), lambda i: (i, 0))
    return pl.pallas_call(
        update_kernel,
        grid=(4,),
        out_shape=(jax.ShapeDtypeStruct((512, 1024), F32),) * 2,
        in_specs=[pl.BlockSpec((8, 128), lambda i: (0, 0)), block, block, block],
        out_specs=(block, block),
    )(trust, wg, weight, velocity)


def per_device(view_features, weight, velocity):
    wg, trust = gradient(view_features, weight)
    return update(trust, wg, weight, velocity)


def solution(mesh):
    in_specs = (P(None, "dp", "feat"), P("dp", "feat"), P("dp", "feat"))
    out_specs = (P("dp", "feat"), P("dp", "feat"))
    return jax.shard_map(
        per_device, mesh=mesh, in_specs=in_specs, out_specs=out_specs, check_vma=False
    )
```

time: 237 us -> 205 us (0.86)
  Pallas kernels: 229 us -> 204 us
  other arithmetic: 6.07 us -> 0 us
    pallas_call x2, Pallas kernels: 229 us -> 204 us  [the longest x1 198 us: gradient(): pl.pallas_call(kernel, out_shape=(jax.ShapeDtypeStruct((512, 1024), F32),...]
    sub x1 -> x0, other arithmetic: 6.07 us -> none  [per_device(): return (weight - LEARN_RATE * new_velocity, new_velocity)]
where the time goes in v3:
time: 205 us; the launch traced here: 204 us
  Pallas kernels  204 us (100%)
    pallas_call x1, Pallas kernels, gradient(): pl.pallas_call(kernel, out_shape=(jax.ShapeDtypeStruct((512, 1024), F32),...  198 us
    pallas_call x1, Pallas kernels, update(): pl.pallas_call(update_kernel, grid=(4,), out_shape=(jax.ShapeDtypeStruct(...  5.4 us

profile of v3, /device:TPU:1, one launch (start us, length us, event | category | flops | bytes accessed | tf_op | source)
XLA Modules:
  0.0 204.3 jit_solution(5157248275187379093)
XLA Ops:
  0.6 198.3 %shard_map.50 = (f32[512,1024]{1,0:T(8,128)}, f32[8,128]{1,0:T(8,128)}) custom-call(bf16[2,128,1024]{2,1,0:T(8,128)(2,1)} %x_ref.1, f32[512,1024]{1,0:T(8,128)} %w_ref.3), custom_call_target="tpu_custom_call" | custom-call | tf_op jit(solution)/shard_map/pallas_call | solution.py:447
  198.9 5.4 %shard_map.51 = (f32[512,1024]{1,0:T(8,128)}, f32[512,1024]{1,0:T(8,128)}) custom-call(f32[8,128]{1,0:T(8,128)} %get-tuple-element.4.trust_ref, f32[512,1024]{1,0:T(8,128)} %get-tuple-element.5.wg_ref, f32[512,1024]{1,0:T(8,128)} %w_ref.3, f32[512,1024]{1,0:T(8,128)} %v_ref.1), custom_call_target="tpu_custom_call" | custom-call | tf_op jit(solution)/shard_map/pallas_call | solution.py:479

commit v4 on v3

--- a/solution.py
+++ b/solution.py
@@ -143,9 +143,9 @@
 
 def kernel(
     x_ref, w_ref, wg_ref, trust_ref,
-    st, xg, wf, ys, yr, zs, zr, yacc, normed_ref, half_ref,
+    st, xg, wf, ys, via, yr, zs, zr, yacc, normed_ref, half_ref,
     hg, hother, gs, gr, gzs, gzr, gram, ts, tr, og, wacc, wrecv, msg, got, mid, got2,
-    p1_s, p1_r, p2_s, p2_r, v_s, v_r, ag_s, ag_r, rs_s, rs_r, z_s, z_r,
+    p1_s, p1_r, p2_s, p2_r, v_s, v_r, ag_s, ag_r, via_s, via_r, rs_s, rs_r, z_s, z_r,
     c_s, c_r, h_s, h_r, g_s, g_r, gz_s, gz_r, gg_s, gg_r, t_s, t_r, o_s, o_r, w_s, w_r, n_s, n_r, m_s, m_r,
 ):
     me = Place()
@@ -166,60 +166,64 @@
 
     pl.semaphore_wait(pltpu.get_barrier_semaphore(), len(partners) + jnp.where(still, 0, 1))
 
-    phase1 = []
-    for dj in (2, 1, 3, 0):
-        for dv in (0, 1):
-            v, j = (c + dv) % 2, (y + dj) % 4
-            src = x_ref.at[v, aligned(j, 32)]
-            dst = st.at[y, aligned(c, 32)]
-            if dj == 0 and dv == 0:
-                own = pltpu.make_async_copy(src, dst, p1_r.at[0, 0])
-                own.start()
-            else:
-                copy = remote(src, dst, p1_s.at[dj, dv], p1_r.at[dj, dv], me.at(c=v, y=j))
+    phase1, owns = [[], []], []
+    for half in range(2):
+        for dj in (2, 1, 3, 0):
+            for dv in (0, 1):
+                v, j = (c + dv) % 2, (y + dj) % 4
+                src = x_ref.at[v, pl.ds(pl.multiple_of(j * 32 + half * 16, 16), 16)]
+                dst = st.at[y, pl.ds(pl.multiple_of(half * 32 + c * 16, 16), 16)]
+                if dj == 0 and dv == 0:
+                    copy = pltpu.make_async_copy(src, dst, p1_r.at[half, 0, 0])
+                    owns.append(copy)
+                else:
+                    copy = remote(
+                        src, dst, p1_s.at[half, dj, dv], p1_r.at[half, dj, dv], me.at(c=v, y=j)
+                    )
+                    phase1[half].append(copy)
                 copy.start()
-                phase1.append((dj, dv, copy))
     own_rows = aligned(c, 512)
     wf[own_rows, :] = w_ref[...].astype(BF)
     wcopy = remote(wf.at[own_rows], wf.at[own_rows], v_s, v_r, me.at(c=1 - c))
     wcopy.start()
-    for dj, dv, copy in phase1:
-        copy.wait_recv()
-    own.wait()
-
-    landing = pl.ds(pl.multiple_of((zh * 4 + y) * 256 + x * 64, 64), 64)
-    phase2 = []
-    for dx in (2, 1, 3, 0):
-        xt = (x + dx) % 4
-        phase2.append(remote(
-            st.at[xt], xg.at[landing], p2_s.at[dx], p2_r.at[x], me.at(zh=zl, x=xt, zl=zh)
-        ))
-        if dx == 0:
-            @pl.when(still)
-            def _():
-                pltpu.make_async_copy(st.at[x], xg.at[landing], p2_r.at[x]).start()
-
-            @pl.when(jnp.logical_not(still))
-            def _():
-                phase2[-1].start()
-        else:
-            phase2[-1].start()
+    phase2 = [[], []]
+    for half in range(2):
+        for copy in phase1[half]:
+            copy.wait_recv()
+        owns[half].wait()
+        landing = pl.ds(pl.multiple_of((zh * 4 + y) * 256 + half * 128 + x * 32, 32), 32)
+        part = pl.ds(half * 32, 32)
+        for dx in (2, 1, 3, 0):
+            xt = (x + dx) % 4
+            copy = remote(
+                st.at[xt, part], xg.at[landing], p2_s.at[half, dx], p2_r.at[half, x], me.at(zh=zl, x=xt, zl=zh)
+            )
+            phase2[half].append(copy)
+            if dx == 0:
+                @pl.when(still)
+                def _():
+                    pltpu.make_async_copy(st.at[x, part], xg.at[landing], p2_r.at[half, x]).start()
+
+                @pl.when(jnp.logical_not(still))
+                def _():
+                    copy.start()
+            else:
+                copy.start()
 
     ag = Gather(
         zl, y, lambda q, r: me.at(zl=q, y=r),
         lambda b, k: xg.at[pl.ds(pl.multiple_of(b * 256 + k * 64, 64), 64)], ag_s, ag_r,
     )
-    for k in range(NCH):
-        ref = xg.at[pl.ds(pl.multiple_of(f * 256 + k * 64, 64), 64)]
-        pltpu.make_async_copy(ref, ref, p2_r.at[k]).wait()
-        ag.own(k)
-    wcopy.wait_recv()
-
     order = [f] + ag.blocks
-    sends = []
-
-    def product(o):
-        rows = aligned(order[o], 256)
+    up, down, far = (x + 1) % 4, (x + 3) % 4, (x + 2) % 4
+    units, via_copies, ring_copies, zcopies = [], [], [], []
+
+    def span(o, h, size=128, at=0):
+        return pl.ds(pl.multiple_of(order[o] * 256 + (h * 128 + at), 64), size)
+
+    def product(o, h):
+        u = len(units)
+        rows = span(o, h)
 
         @pl.loop(0, 4)
         def _(j):
@@ -227,47 +231,91 @@
             ys[2 * (j % 2), j // 2, rows, :] = part[:, :128]
             ys[2 * (j % 2) + 1, j // 2, rows, :] = part[:, 128:]
 
-        for dx in (2, 1, 3):
-            xt = (x + dx) % 4
+        pair = []
+        for way, to in ((0, up), (1, down)):
             copy = remote(
-                ys.at[xt, :, rows], yr.at[dx - 1, :, rows], rs_s.at[dx - 1, o], rs_r.at[dx - 1, o], me.at(x=xt)
+                ys.at[far, :, span(o, h, 64, 64 * way)], via.at[way, :, pl.ds(u * 64, 64)],
+                via_s.at[way, u], via_r.at[way, u], me.at(x=to),
             )
             copy.start()
-            sends.append(copy)
-
-    product(0)
-    for k in range(NCH):
-        ag.near(k)
-    product(1)
-    product(2)
-    product(3)
-    for k in range(NCH):
-        ag.far(k)
-    product(4)
-    for k in range(NCH):
-        ag.rest(k)
-    product(5)
-    product(6)
-    for k in range(NCH):
-        ag.last(k)
-    product(7)
-    zcopies = []
-    for o in range(8):
-        rows = aligned(order[o], 256)
-        for copy in sends[3 * o:3 * o + 3]:
+            pair.append(copy)
+        units.append((o, h))
+        via_copies.append(pair)
+
+    def pass_on(u):
+        o, h = units[u]
+        rows = span(o, h)
+        pair = []
+        for way, to in ((0, up), (1, down)):
+            via_copies[u][way].wait_recv()
+            part = span(o, h, 64, 64 * way)
+            for side in range(2):
+                ys[to, side, part, :] = (
+                    ys[to, side, part, :].astype(F32) + via[way, side, pl.ds(u * 64, 64), :].astype(F32)
+                ).astype(BF)
+            copy = remote(
+                ys.at[to, :, rows], yr.at[way, :, rows], rs_s.at[way, u], rs_r.at[way, u], me.at(x=to)
+            )
+            copy.start()
+            pair.append(copy)
+        ring_copies.append(pair)
+
+    def settle(u):
+        rows = span(*units[u])
+        for copy in ring_copies[u]:
             copy.wait_recv()
 
         def total(side):
             s = ys[x, side, rows, :].astype(F32)
-            for i in range(3):
-                s = s + yr[i, side, rows, :].astype(F32)
-            return s
+            return s + yr[0, side, rows, :].astype(F32) + yr[1, side, rows, :].astype(F32)
 
         zs[rows, :] = total(1 - zh).astype(BF)
-        copy = remote(zs.at[rows], zr.at[rows], z_s.at[o], z_r.at[o], me.at(zh=1 - zh))
+        copy = remote(zs.at[rows], zr.at[rows], z_s.at[u], z_r.at[u], me.at(zh=1 - zh))
         copy.start()
         zcopies.append(copy)
         yacc[rows, :] = total(zh)
+
+    def push(o, h):
+        product(o, h)
+        u = len(units) - 1
+        if u >= 1:
+            pass_on(u - 1)
+        if u >= 4:
+            settle(u - 4)
+
+    for k in range(NCH):
+        for i in range(2):
+            ref = xg.at[pl.ds(pl.multiple_of(f * 256 + k * 64 + i * 32, 32), 32)]
+            pltpu.make_async_copy(ref, ref, p2_r.at[k // 2, 2 * (k % 2) + i]).wait()
+        ag.own(k)
+        if k == 1:
+            wcopy.wait_recv()
+            push(0, 0)
+    push(0, 1)
+    for h in range(2):
+        for k in (2 * h, 2 * h + 1):
+            ag.near(k)
+        for o in (1, 2, 3):
+            push(o, h)
+    for step in ((0, 1), (2, 3)):
+        h = step[0] // 2
+        for k in step:
+            ag.far(k)
+        push(4, h)
+        if h == 1:
+            ag.last(0)
+            ag.last(1)
+            push(7, 0)
+        for k in step:
+            ag.rest(k)
+        push(5, h)
+        push(6, h)
+    ag.last(2)
+    ag.last(3)
+    push(7, 1)
+    pass_on(15)
+    for u in range(12, 16):
+        settle(u)
     for copy in zcopies:
         copy.wait_recv()
     outputs = yacc[...] + zr[...].astype(F32)
@@ -333,21 +381,31 @@
     gg.run()
 
     kappa = 2.0 * REDUNDANCY / (n * n)
-    for j in range(4):
-        part = kappa * jnp.dot(gram[...], hg[:, pl.ds(j * 256, 256)], preferred_element_type=F32)
-        ts[2 * j] = part[:, :128].astype(BF)
-        ts[2 * j + 1] = part[:, 128:].astype(BF)
     tcopies = []
-    for i in (2, 6, 5, 4, 3, 1, 7):
-        to = (mine + i) % 8
-        copy = remote(
-            ts.at[to], tr.at[aligned(mine, 256)], t_s.at[i - 1], t_r.at[i - 1], me.along(to)
-        )
-        copy.start()
-        tcopies.append(copy)
+    member = mine % 2
+    for i in (2, 1, 3, 0):
+        tile = (mine // 2 + i) % 4
+        part = kappa * jnp.dot(gram[...], hg[:, aligned(tile, 256)], preferred_element_type=F32)
+        ts[2 * tile] = part[:, :128].astype(BF)
+        ts[2 * tile + 1] = part[:, 128:].astype(BF)
+        for side in range(2):
+            to = 2 * tile + side
+            if i == 0:
+                to = mine + 1 - 2 * member
+            if i != 0 or side == 0:
+                copy = remote(
+                    ts.at[to], tr.at[aligned(mine, 256)], t_s.at[i, side], t_r.at[i, member], me.along(to)
+                )
+                copy.start()
+                tcopies.append(copy)
     tr[aligned(mine, 256), :] = ts[mine]
-    for copy in tcopies:
-        copy.wait_recv()
+    ref = ts.at[0]
+    for i in (0, 1, 2, 3):
+        if i == 0:
+            pltpu.make_async_copy(ref, ref, t_r.at[0, 1 - member]).wait()
+        else:
+            for side in range(2):
+                pltpu.make_async_copy(ref, ref, t_r.at[i, side]).wait()
     grads = tr[...].astype(F32) + extra * hother[...].astype(F32)
     normed = normed_ref[...]
     mean = jnp.sum(grads, 0, keepdims=True) / n
@@ -416,16 +474,15 @@
         s = s + got2[i]
     sums = jnp.sqrt(jnp.sum(s, 1, keepdims=True))
     trust_ref[...] = jnp.broadcast_to(sums[1:2, :] / (sums[0:1, :] + NORM_EPSILON), (8, 128))
-    for copy in [swap, gzcopy, gcopy, wcopy] + sends + zcopies + gcopies + tcopies + ncopies + mcopies:
+    for copy in [swap, gzcopy, gcopy, wcopy] + sum(via_copies + ring_copies, []) + zcopies + gcopies + tcopies + ncopies + mcopies:
         copy.wait_send()
-    for dj, dv, copy in phase1:
-        copy.wait_send()
-    for copy in phase2[:3]:
+    for copy in phase1[0] + phase1[1] + phase2[0][:3] + phase2[1][:3]:
         copy.wait_send()
 
     @pl.when(jnp.logical_not(still))
     def _():
-        phase2[3].wait_send()
+        phase2[0][3].wait_send()
+        phase2[1][3].wait_send()
 
     for g in (ag, hh, gg, oo):
         g.close()
@@ -453,14 +510,14 @@
         in_specs=vmem(2),
         out_specs=tuple(vmem(2)),
         scratch_shapes=[
-            v(4, 64, 1024), v(2048, 1024), v(1024, 1024), v(4, 2, 2048, 128), v(3, 2, 2048, 128),
+            v(4, 64, 1024), v(2048, 1024), v(1024, 1024), v(4, 2, 2048, 128), v(2, 2, 1024, 128), v(2, 2, 2048, 128),
             v(2048, 128), v(2048, 128), v(2048, 128, kind=F32), v(2048, 128, kind=F32), v(2048, 128),
             v(2048, 1024), v(2048, 128), v(4, 2, 256, 256), v(4, 2, 256, 256), v(256, 256), v(256, 256),
             v(256, 2048), v(8, 256, 128), v(2048, 128), v(2048, 1024), v(1024, 1024, kind=F32),
             v(512, 1024, kind=F32), v(8, 128, kind=F32), v(15, 8, 128, kind=F32), v(8, 128, kind=F32),
             v(7, 8, 128, kind=F32),
-            *two(4, 2), *two(4), *two(), *two(7, NCH), *two(3, 8), *two(8),
-            *two(), *two(7, NCH), *two(4), *two(), *two(7, 2), *two(7), *two(7, NCH), *two(), *two(15), *two(7),
+            *two(2, 4, 2), *two(2, 4), *two(), *two(7, NCH), *two(2, 16), *two(2, 16), *two(16),
+            *two(), *two(7, NCH), *two(4), *two(), *two(7, 2), *two(4, 2), *two(7, NCH), *two(), *two(15), *two(7),
         ],
         compiler_params=pltpu.CompilerParams(
             collective_id=0, has_side_effects=True, vmem_limit_bytes=60 * 2**20

time: 205 us -> 193 us (0.941)
  Pallas kernels: 204 us -> 192 us
    pallas_call x1, Pallas kernels: 198 us -> 187 us  [gradient(): pl.pallas_call(kernel, out_shape=(jax.ShapeDtypeStruct((512, 1024), F32),...]
where the time goes in v4:
time: 193 us
  Pallas kernels  192 us (99%)
    pallas_call x1, Pallas kernels, gradient(): pl.pallas_call(kernel, out_shape=(jax.ShapeDtypeStruct((512, 1024), F32),...  187 us
    pallas_call x1, Pallas kernels, update(): pl.pallas_call(update_kernel, grid=(4,), out_shape=(jax.ShapeDtypeStruct(...  5.4 us

profile of v4, /device:TPU:1, one launch (start us, length us, event | category | flops | bytes accessed | tf_op | source)
XLA Modules:
  0.0 192.8 jit_solution(17275919399190513431)
XLA Ops:
  0.6 186.7 %shard_map.50 = (f32[512,1024]{1,0:T(8,128)}, f32[8,128]{1,0:T(8,128)}) custom-call(bf16[2,128,1024]{2,1,0:T(8,128)(2,1)} %x_ref.1, f32[512,1024]{1,0:T(8,128)} %w_ref.3), custom_call_target="tpu_custom_call" | custom-call | tf_op jit(solution)/shard_map/pallas_call | solution.py:504
  187.4 5.4 %shard_map.51 = (f32[512,1024]{1,0:T(8,128)}, f32[512,1024]{1,0:T(8,128)}) custom-call(f32[8,128]{1,0:T(8,128)} %get-tuple-element.4.trust_ref, f32[512,1024]{1,0:T(8,128)} %get-tuple-element.5.wg_ref, f32[512,1024]{1,0:T(8,128)} %w_ref.3, f32[512,1024]{1,0:T(8,128)} %v_ref.1), custom_call_target="tpu_custom_call" | custom-call | tf_op jit(solution)/shard_map/pallas_call | solution.py:536

commit v5 on v4

--- a/solution.py
+++ b/solution.py
@@ -101,10 +101,13 @@
         first = 1 + k % 2
         c[first].wait_recv()
         c[3].start()
+        c[3 - first].wait_recv()
+
+    def turn(self, k):
+        c = self.copies[k]
         c[0].wait_recv()
         c[4].start()
         c[5].start()
-        c[3 - first].wait_recv()
 
     def far(self, k):
         c = self.copies[k]
@@ -127,7 +130,7 @@
         self.copies[k][6].wait_recv()
 
     def run(self):
-        for step in (self.own, self.near, self.far, self.rest, self.last):
+        for step in (self.own, self.near, self.turn, self.far, self.rest, self.last):
             for k in range(self.count):
                 step(k)
 
@@ -295,6 +298,7 @@
     for h in range(2):
         for k in (2 * h, 2 * h + 1):
             ag.near(k)
+            ag.turn(k)
         for o in (1, 2, 3):
             push(o, h)
     for step in ((0, 1), (2, 3)):
@@ -338,7 +342,7 @@
     swap = remote(half_ref, hother, c_s, c_r, me.at(c=1 - c))
     swap.start()
     squares = jnp.sum(w_ref[...] * w_ref[...], 0, keepdims=True)
-    for step in (hh.near, hh.far, hh.rest, hh.last):
+    for step in (hh.near, hh.turn, hh.far, hh.rest, hh.last):
         for k in range(NCH):
             step(k)
 
@@ -416,7 +420,7 @@
         zh, x, lambda q, r: me.at(zh=q, x=r),
         lambda b, k: og.at[pl.ds(k * 512, 512), aligned(b, 128)], o_s, o_r,
     )
-    for step in (oo.own, oo.near, oo.far):
+    for step in (oo.own, oo.near, oo.turn, oo.far):
         for k in range(NCH):
             step(k)
     gcopy = remote(wacc.at[aligned(1 - c, 512)], wrecv, w_s, w_r, me.at(c=1 - c))
@@ -532,10 +536,10 @@
 
 
 def update(trust, wg, weight, velocity):
-    block = pl.BlockSpec((128, 1024), lambda i: (i, 0))
+    block = pl.BlockSpec((256, 1024), lambda i: (i, 0))
     return pl.pallas_call(
         update_kernel,
-        grid=(4,),
+        grid=(2,),
         out_shape=(jax.ShapeDtypeStruct((512, 1024), F32),) * 2,
         in_specs=[pl.BlockSpec((8, 128), lambda i: (0, 0)), block, block, block],
         out_specs=(block, block),

time: 193 us -> 190 us (0.984)
  Pallas kernels: 192 us -> 189 us
    pallas_call x1, Pallas kernels: 187 us -> 184 us  [gradient(): pl.pallas_call(kernel, out_shape=(jax.ShapeDtypeStruct((512, 1024), F32),...]
where the time goes in v5:
time: 190 us
  Pallas kernels  189 us (99%)
    pallas_call x1, Pallas kernels, gradient(): pl.pallas_call(kernel, out_shape=(jax.ShapeDtypeStruct((512, 1024), F32),...  184 us
    pallas_call x1, Pallas kernels, update(): pl.pallas_call(update_kernel, grid=(2,), out_shape=(jax.ShapeDtypeStruct(...  4.61 us

profile of v5, /device:TPU:1, one launch (start us, length us, event | category | flops | bytes accessed | tf_op | source)
XLA Modules:
  0.0 189.6 jit_solution(8823784232847144510)
XLA Ops:
  0.6 184.4 %shard_map.50 = (f32[512,1024]{1,0:T(8,128)}, f32[8,128]{1,0:T(8,128)}) custom-call(bf16[2,128,1024]{2,1,0:T(8,128)(2,1)} %x_ref.1, f32[512,1024]{1,0:T(8,128)} %w_ref.3), custom_call_target="tpu_custom_call" | custom-call | tf_op jit(solution)/shard_map/pallas_call | solution.py:508
  185.0 4.6 %shard_map.51 = (f32[512,1024]{1,0:T(8,128)}, f32[512,1024]{1,0:T(8,128)}) custom-call(f32[8,128]{1,0:T(8,128)} %get-tuple-element.4.trust_ref, f32[512,1024]{1,0:T(8,128)} %get-tuple-element.5.wg_ref, f32[512,1024]{1,0:T(8,128)} %w_ref.3, f32[512,1024]{1,0:T(8,128)} %v_ref.1), custom_call_target="tpu_custom_call" | custom-call | tf_op jit(solution)/shard_map/pallas_call | solution.py:540

commit v6 on v5

--- a/solution.py
+++ b/solution.py
@@ -155,8 +155,12 @@
     d, p, f, c, x, y, zh, zl = me.d, me.p, me.f, me.c, me.x, me.y, me.zh, me.zl
     n = 2048
     still = zh == zl
-    partners = [((d + i) % 16, f) for i in range(1, 16)]
-    partners += [(d, (f + i) % 8) for i in range(1, 8)]
+    same_feat = [
+        me.at(zh=(zh + i) % 2, x=(x + j) % 4, c=(c + k) % 2)
+        for i in (1, 0) for j in (2, 1, 3, 0) for k in (0, 1)
+    ][:-2] + [me.at(c=1 - c)]
+    same_dp = [me.at(zl=(zl + i) % 2, y=(y + j) % 4) for i in (1, 0) for j in (2, 1, 3, 0)][:-1]
+    partners = same_feat + same_dp
     partners += [me.at(c=1 - c, y=(y + i) % 4) for i in range(1, 4)]
     partners += [me.at(zh=zl, x=(x + i) % 4, zl=zh) for i in range(1, 4)]
     mirror = me.at(zh=zl, zl=zh)
@@ -327,18 +331,19 @@
     centered = outputs - average
     variance = jnp.sum(centered * centered, 0, keepdims=True) / n
     inverse = lax.rsqrt(variance + EPSILON)
-    normed = centered * inverse
-    normed_ref[...] = normed
-    half_ref[...] = normed.astype(BF)
 
     mine, crossing = jnp.where(c == 0, p, f), jnp.where(c == 0, f, p)
-    hg[:, aligned(mine, 128)] = normed.astype(BF)
     hh = Gather(
         mine // 4, mine % 4, lambda q, r: me.along(q * 4 + r),
         lambda b, k: hg.at[pl.ds(k * 512, 512), aligned(b, 128)], h_s, h_r, NCH, (1,),
     )
     for k in range(NCH):
+        rows = slice(k * 512, (k + 1) * 512)
+        normed = centered[rows] * inverse
+        hg[rows, aligned(mine, 128)] = normed.astype(BF)
         hh.own(k)
+        normed_ref[rows, :] = normed
+        half_ref[rows, :] = normed.astype(BF)
     swap = remote(half_ref, hother, c_s, c_r, me.at(c=1 - c))
     swap.start()
     squares = jnp.sum(w_ref[...] * w_ref[...], 0, keepdims=True)
@@ -346,34 +351,37 @@
         for k in range(NCH):
             step(k)
 
-    gcopies = []
-    for i in (2, 1, 3, 0):
-        t = (crossing + i) % 4
-        for side in range(2):
-            gs[t, side] = lax.dot_general(
-                hg[aligned(side * 4 + t, 256), :], hg[aligned(mine, 256), :],
-                (((1,), (1,)), ((), ())), preferred_element_type=F32,
-            ).astype(BF)
-        copy = remote(
-            gs.at[t], gr.at[i], g_s.at[i], g_r.at[i], me.across_swapped((crossing // 4) * 4 + t)
-        )
-        copy.start()
-        gcopies.append(copy)
+    gcopies = [[], []]
+    for step in range(2):
+        side = (1 - crossing // 4) if step == 0 else crossing // 4
+        gs[side] = lax.dot_general(
+            hg[aligned(side, 1024), :], hg[aligned(mine, 256), :],
+            (((1,), (1,)), ((), ())), preferred_element_type=F32,
+        ).astype(BF).reshape(4, 256, 256)
+        for i in (2, 1, 3, 0):
+            t = (crossing + i) % 4
+            copy = remote(
+                gs.at[side, t], gr.at[i, side], g_s.at[step, i], g_r.at[step, i],
+                me.across_swapped((crossing // 4) * 4 + t),
+            )
+            copy.start()
+            gcopies[step].append(copy)
     swap.wait_recv()
     corr = jnp.sum(half_ref[...].astype(F32) * hother[...].astype(F32), 0, keepdims=True) / n
     extra = (-2.0 * (1.0 - corr) - 2.0 * REDUNDANCY * corr) / n
-    for copy in gcopies:
-        copy.wait_recv()
     q = mine // 4
+    other = 1 - q
 
     def gram_total(side):
+        for copy in gcopies[0 if side is other else 1]:
+            copy.wait_recv()
         s = gr[0, side].astype(F32)
         for i in range(1, 4):
             s = s + gr[i, side].astype(F32)
         return s
 
-    gzs[...] = gram_total(1 - q).astype(BF)
-    gzcopy = remote(gzs, gzr, gz_s, gz_r, me.along((1 - q) * 4 + mine % 4))
+    gzs[...] = gram_total(other).astype(BF)
+    gzcopy = remote(gzs, gzr, gz_s, gz_r, me.along(other * 4 + mine % 4))
     gzcopy.start()
     keep = gram_total(q)
     gzcopy.wait_recv()
@@ -414,37 +422,51 @@
     normed = normed_ref[...]
     mean = jnp.sum(grads, 0, keepdims=True) / n
     cross = jnp.sum(grads * normed, 0, keepdims=True) / n
-    og[:, aligned(p, 128)] = (inverse * (grads - mean - normed * cross)).astype(BF)
 
     oo = Gather(
         zh, x, lambda q, r: me.at(zh=q, x=r),
         lambda b, k: og.at[pl.ds(k * 512, 512), aligned(b, 128)], o_s, o_r,
     )
-    for step in (oo.own, oo.near, oo.turn, oo.far):
+    for k in range(NCH):
+        rows = slice(k * 512, (k + 1) * 512)
+        og[rows, aligned(p, 128)] = (inverse * (grads[rows] - mean - normed[rows] * cross)).astype(BF)
+        oo.own(k)
+    for step in (oo.near, oo.turn, oo.far):
         for k in range(NCH):
             step(k)
-    gcopy = remote(wacc.at[aligned(1 - c, 512)], wrecv, w_s, w_r, me.at(c=1 - c))
+    near_cols, far_cols = aligned(zh, 512), aligned(1 - zh, 512)
+
+    @pl.loop(0, 4)
+    def _(m):
+        cols = aligned(m, 256)
+        wacc[cols, near_cols] = lax.dot_general(
+            xg[:, cols], og[:, near_cols], (((0,), (0,)), ((), ())), preferred_element_type=F32
+        )
+
+    gcopies2 = []
     for k in range(NCH):
         oo.rest(k)
         oo.last(k)
         rows = pl.ds(k * 512, 512)
         for side in range(2):
             core = (1 - c) if side == 0 else c
-
-            @pl.loop(0, 2)
-            def _(m):
+            for m in range(2):
                 cols = aligned(core * 2 + m, 256)
                 part = lax.dot_general(
-                    xg[rows, cols], og[rows, :], (((0,), (0,)), ((), ())), preferred_element_type=F32
+                    xg[rows, cols], og[rows, far_cols], (((0,), (0,)), ((), ())), preferred_element_type=F32
                 )
                 if k == 0:
-                    wacc[cols, :] = part
+                    wacc[cols, far_cols] = part
                 else:
-                    wacc[cols, :] += part
-
-            if k == NCH - 1 and side == 0:
-                gcopy.start()
-    gcopy.wait_recv()
+                    wacc[cols, far_cols] += part
+                if k == NCH - 1 and side == 0:
+                    copy = remote(
+                        wacc.at[cols], wrecv.at[pl.ds(m * 256, 256)], w_s.at[m], w_r.at[m], me.at(c=1 - c)
+                    )
+                    copy.start()
+                    gcopies2.append(copy)
+    for copy in gcopies2:
+        copy.wait_recv()
     wg = wacc[aligned(c, 512), :] + wrecv[...]
     wg_ref[...] = wg
     grad_squares = jnp.sum(wg * wg, 0, keepdims=True)
@@ -459,8 +481,8 @@
     msg[0:1, :] = fold(grad_squares)
     msg[1:2, :] = fold(squares)
     ncopies = []
-    for i in range(1, 16):
-        copy = remote(msg, got.at[i - 1], n_s.at[i - 1], n_r.at[i - 1], ((d + i) % 16, f))
+    for i, to in enumerate(same_feat):
+        copy = remote(msg, got.at[i], n_s.at[i], n_r.at[i], to)
         copy.start()
         ncopies.append(copy)
     s = msg[...]
@@ -469,8 +491,8 @@
         s = s + got[i]
     mid[...] = s
     mcopies = []
-    for i in range(1, 8):
-        copy = remote(mid, got2.at[i - 1], m_s.at[i - 1], m_r.at[i - 1], (d, (f + i) % 8))
+    for i, to in enumerate(same_dp):
+        copy = remote(mid, got2.at[i], m_s.at[i], m_r.at[i], to)
         copy.start()
         mcopies.append(copy)
     for i, copy in enumerate(mcopies):
@@ -478,7 +500,7 @@
         s = s + got2[i]
     sums = jnp.sqrt(jnp.sum(s, 1, keepdims=True))
     trust_ref[...] = jnp.broadcast_to(sums[1:2, :] / (sums[0:1, :] + NORM_EPSILON), (8, 128))
-    for copy in [swap, gzcopy, gcopy, wcopy] + sum(via_copies + ring_copies, []) + zcopies + gcopies + tcopies + ncopies + mcopies:
+    for copy in [swap, gzcopy, wcopy] + gcopies2 + sum(via_copies + ring_copies, []) + zcopies + gcopies[0] + gcopies[1] + tcopies + ncopies + mcopies:
         copy.wait_send()
     for copy in phase1[0] + phase1[1] + phase2[0][:3] + phase2[1][:3]:
         copy.wait_send()
@@ -516,12 +538,12 @@
         scratch_shapes=[
             v(4, 64, 1024), v(2048, 1024), v(1024, 1024), v(4, 2, 2048, 128), v(2, 2, 1024, 128), v(2, 2, 2048, 128),
             v(2048, 128), v(2048, 128), v(2048, 128, kind=F32), v(2048, 128, kind=F32), v(2048, 128),
-            v(2048, 1024), v(2048, 128), v(4, 2, 256, 256), v(4, 2, 256, 256), v(256, 256), v(256, 256),
+            v(2048, 1024), v(2048, 128), v(2, 4, 256, 256), v(4, 2, 256, 256), v(256, 256), v(256, 256),
             v(256, 2048), v(8, 256, 128), v(2048, 128), v(2048, 1024), v(1024, 1024, kind=F32),
             v(512, 1024, kind=F32), v(8, 128, kind=F32), v(15, 8, 128, kind=F32), v(8, 128, kind=F32),
             v(7, 8, 128, kind=F32),
             *two(2, 4, 2), *two(2, 4), *two(), *two(7, NCH), *two(2, 16), *two(2, 16), *two(16),
-            *two(), *two(7, NCH), *two(4), *two(), *two(7, 2), *two(4, 2), *two(7, NCH), *two(), *two(15), *two(7),
+            *two(), *two(7, NCH), *two(2, 4), *two(), *two(7, 2), *two(4, 2), *two(7, NCH), *two(2), *two(15), *two(7),
         ],
         compiler_params=pltpu.CompilerParams(
             collective_id=0, has_side_effects=True, vmem_limit_bytes=60 * 2**20

time: 190 us -> 187 us (0.984)
  Pallas kernels: 189 us -> 186 us
    pallas_call x1, Pallas kernels: 184 us -> 182 us  [gradient(): pl.pallas_call(kernel, out_shape=(jax.ShapeDtypeStruct((512, 1024), F32),...]
where the time goes in v6:
time: 187 us
  Pallas kernels  186 us (99%)
    pallas_call x1, Pallas kernels, gradient(): pl.pallas_call(kernel, out_shape=(jax.ShapeDtypeStruct((512, 1024), F32),...  182 us
    pallas_call x1, Pallas kernels, update(): pl.pallas_call(update_kernel, grid=(2,), out_shape=(jax.ShapeDtypeStruct(...  4.61 us

profile of v6, /device:TPU:1, one launch (start us, length us, event | category | flops | bytes accessed | tf_op | source)
XLA Modules:
  0.0 187.0 jit_solution(13612604298629057179)
XLA Ops:
  0.6 181.8 %shard_map.50 = (f32[512,1024]{1,0:T(8,128)}, f32[8,128]{1,0:T(8,128)}) custom-call(bf16[2,128,1024]{2,1,0:T(8,128)(2,1)} %x_ref.1, f32[512,1024]{1,0:T(8,128)} %w_ref.3), custom_call_target="tpu_custom_call" | custom-call | tf_op jit(solution)/shard_map/pallas_call | solution.py:530
  182.4 4.6 %shard_map.51 = (f32[512,1024]{1,0:T(8,128)}, f32[512,1024]{1,0:T(8,128)}) custom-call(f32[8,128]{1,0:T(8,128)} %get-tuple-element.4.trust_ref, f32[512,1024]{1,0:T(8,128)} %get-tuple-element.5.wg_ref, f32[512,1024]{1,0:T(8,128)} %w_ref.3, f32[512,1024]{1,0:T(8,128)} %v_ref.1), custom_call_target="tpu_custom_call" | custom-call | tf_op jit(solution)/shard_map/pallas_call | solution.py:562

commit v7 on v6

--- a/solution.py
+++ b/solution.py
@@ -386,11 +386,25 @@
     keep = gram_total(q)
     gzcopy.wait_recv()
     gram[:, aligned(crossing, 256)] = (keep + gzr[...].astype(F32)).astype(BF)
-    gg = Gather(
-        crossing // 4, crossing % 4, lambda q, r: me.across(q * 4 + r),
-        lambda b, k: gram.at[pl.ds(k * 128, 128), aligned(b, 256)], gg_s, gg_r, 2, (),
-    )
-    gg.run()
+    qc, rc = crossing // 4, crossing % 4
+    pair_block = (1 - qc) * 4 + rc
+    gg = []
+    for k in range(2):
+        chunk = []
+        for slot in range(7):
+            to = pair_block if slot == 0 else qc * 4 + (rc + (2, 1, 3)[(slot - 1) % 3]) % 4
+            ref = gram.at[pl.ds(k * 128, 128), aligned(crossing if slot < 4 else pair_block, 256)]
+            chunk.append(remote(ref, ref, gg_s.at[slot, k], gg_r.at[slot, k], me.across(to)))
+        gg.append(chunk)
+        for slot in range(4):
+            chunk[slot].start()
+    for chunk in gg:
+        chunk[0].wait_recv()
+        for slot in (4, 5, 6):
+            chunk[slot].start()
+    for chunk in gg:
+        for slot in range(1, 7):
+            chunk[slot].wait_recv()
 
     kappa = 2.0 * REDUNDANCY / (n * n)
     tcopies = []
@@ -500,7 +514,7 @@
         s = s + got2[i]
     sums = jnp.sqrt(jnp.sum(s, 1, keepdims=True))
     trust_ref[...] = jnp.broadcast_to(sums[1:2, :] / (sums[0:1, :] + NORM_EPSILON), (8, 128))
-    for copy in [swap, gzcopy, wcopy] + gcopies2 + sum(via_copies + ring_copies, []) + zcopies + gcopies[0] + gcopies[1] + tcopies + ncopies + mcopies:
+    for copy in [swap, gzcopy, wcopy] + gcopies2 + sum(via_copies + ring_copies, []) + zcopies + gcopies[0] + gcopies[1] + sum(gg, []) + tcopies + ncopies + mcopies:
         copy.wait_send()
     for copy in phase1[0] + phase1[1] + phase2[0][:3] + phase2[1][:3]:
         copy.wait_send()
@@ -510,7 +524,7 @@
         phase2[0][3].wait_send()
         phase2[1][3].wait_send()
 
-    for g in (ag, hh, gg, oo):
+    for g in (ag, hh, oo):
         g.close()
 
 

time: 187 us -> 185 us (0.989)
  Pallas kernels: 186 us -> 184 us
    pallas_call x1, Pallas kernels: 182 us -> 180 us  [gradient(): pl.pallas_call(kernel, out_shape=(jax.ShapeDtypeStruct((512, 1024), F32),...]
where the time goes in v7:
time: 185 us
  Pallas kernels  184 us (99%)
    pallas_call x1, Pallas kernels, gradient(): pl.pallas_call(kernel, out_shape=(jax.ShapeDtypeStruct((512, 1024), F32),...  180 us
    pallas_call x1, Pallas kernels, update(): pl.pallas_call(update_kernel, grid=(2,), out_shape=(jax.ShapeDtypeStruct(...  4.61 us

profile of v7, /device:TPU:1, one launch (start us, length us, event | category | flops | bytes accessed | tf_op | source)
XLA Modules:
  0.0 184.8 jit_solution(8497882554674421889)
XLA Ops:
  0.6 179.5 %shard_map.50 = (f32[512,1024]{1,0:T(8,128)}, f32[8,128]{1,0:T(8,128)}) custom-call(bf16[2,128,1024]{2,1,0:T(8,128)(2,1)} %x_ref.1, f32[512,1024]{1,0:T(8,128)} %w_ref.3), custom_call_target="tpu_custom_call" | custom-call | tf_op jit(solution)/shard_map/pallas_call | solution.py:544
  180.2 4.6 %shard_map.51 = (f32[512,1024]{1,0:T(8,128)}, f32[512,1024]{1,0:T(8,128)}) custom-call(f32[8,128]{1,0:T(8,128)} %get-tuple-element.4.trust_ref, f32[512,1024]{1,0:T(8,128)} %get-tuple-element.5.wg_ref, f32[512,1024]{1,0:T(8,128)} %w_ref.3, f32[512,1024]{1,0:T(8,128)} %v_ref.1), custom_call_target="tpu_custom_call" | custom-call | tf_op jit(solution)/shard_map/pallas_call | solution.py:576
